TPU v7x, 32 devices: a whole 2x2x4 slice. The times are simulated.
32 devices in a mesh: ctx: 4 (over z), fsdp: 8 (over y, x, core).
Axes of the slice: x: 2, y: 2, z: 4, core: 2. Of those that a mesh axis runs over, the one named last changes fastest.
Arguments:
- clean: bfloat16 [1024, 5120], P(('ctx', 'fsdp')), may hold values from -6 to 6
- noise: bfloat16 [1024, 5120], P(('ctx', 'fsdp')), may hold values from -6 to 6
- noise_two: bfloat16 [1024, 5120], P(('ctx', 'fsdp')), may hold values from -6 to 6
- steps_gen: int32 [3], replicated, may hold values from 600 to 959
- steps_teacher: int32 [3], replicated, may hold values from 20 to 979
- cache_key: bfloat16 [1024, 4096], P('ctx', 'fsdp'), may hold values from -6 to 6
- cache_value: bfloat16 [1024, 4096], P('ctx', 'fsdp'), may hold values from -6 to 6
- cache_block: int32 [1024], P('ctx'), may hold values from 0 to 6
- span_block: int32 [1], replicated, may hold values from 2 to 6
- gen_query: bfloat16 [5120, 4096], P(None, 'fsdp'), may hold values from -0.07614237 to 0.07614237
- gen_key: bfloat16 [5120, 4096], P(None, 'fsdp'), may hold values from -0.052146567 to 0.052146567
- gen_value: bfloat16 [5120, 4096], P(None, 'fsdp'), may hold values from -0.078125 to 0.078125
- gen_out: bfloat16 [4096, 5120], P('fsdp'), may hold values from -0.375 to 0.375
- teacher_query: bfloat16 [5120, 4096], P(None, 'fsdp'), may hold values from -0.07614237 to 0.07614237
- teacher_key: bfloat16 [5120, 4096], P(None, 'fsdp'), may hold values from -0.052146567 to 0.052146567
- teacher_value: bfloat16 [5120, 4096], P(None, 'fsdp'), may hold values from -0.078125 to 0.078125
- teacher_out: bfloat16 [4096, 5120], P('fsdp'), may hold values from -0.375 to 0.375
Outputs:
- generated: bfloat16 [1024, 5120], P(('ctx', 'fsdp'))
- grad_out: bfloat16 [4096, 5120], P('fsdp')
Inputs may be any that keep to these rules, and one draw needn't show every extreme that they name: span_block holds one id.
All inputs are finite; a program needn't handle non-finite values.
Results may differ from a plain program's by a relative error of at most 0.018.
The roundings to bfloat16 on the way count: a program that leaves them out, or rounds other values in their place, can miss the bound.
Values may be sent and summed in bfloat16 or wider, within the bound.
A program may use at most 128 MiB of HBM per device.

v0:
```python
import jax
import jax.numpy as jnp
from jax import lax
from jax.sharding import PartitionSpec as P

HEAD = 128
FRAMES = 3
STEPS = 1000


SHIFT = 5.0
EPS = 1e-06


def sigmas(steps, offset, count, total):
    level = 1.0 - steps.astype(jnp.float32) / STEPS
    sig = SHIFT * level / (1.0 + (SHIFT - 1.0) * level)
    positions = offset + jnp.arange(count, dtype=jnp.int32)
    frame = positions * FRAMES // total
    match = (frame[:, None] == jnp.arange(FRAMES, dtype=jnp.int32)[None, :]).astype(jnp.float32)
    return jnp.sum(match * sig[None, :], axis=1)[:, None]


def normed(values):
    wide = values.astype(jnp.float32)
    return (wide * lax.rsqrt(jnp.mean(wide * wide, axis=1, keepdims=True) + EPS)).astype(
        jnp.bfloat16
    )


def empty_state(heads, rows, head_size):
    return (
        jnp.full((heads, rows), -1e30, jnp.float32),
        jnp.zeros((heads, rows), jnp.float32),
        jnp.zeros((heads, rows, head_size), jnp.float32),
    )


def absorb(state, query_heads, keys, values, allowed):
    top, total, accum = state
    heads = query_heads.shape[1]
    head_size = query_heads.shape[2]
    count = keys.shape[0]
    key_heads = keys.reshape(count, heads, head_size)
    value_heads = values.reshape(count, heads, head_size)
    scores = jnp.einsum(
        "rhd,phd->hrp", query_heads, key_heads, preferred_element_type=jnp.float32
    ) * (1.0 / head_size**0.5)
    if allowed is None:
        newtop = jnp.maximum(top, jnp.max(scores, axis=2))
        weights = jnp.exp(scores - newtop[:, :, None])
    else:
        visible = (allowed > 0)[None, None, :]
        scores = jnp.where(visible, scores, -1e30)
        newtop = jnp.maximum(top, jnp.max(scores, axis=2))
        weights = jnp.where(visible, jnp.exp(scores - newtop[:, :, None]), 0.0)
    total = jnp.sum(weights, axis=2)
    accum = jnp.einsum(
        "hrp,phd->hrd",
        weights.astype(jnp.bfloat16),
        value_heads,
        preferred_element_type=jnp.float32,
    )
    return (newtop, total, accum)


def finish(state):
    top, total, accum = state
    heads, rows, head_size = accum.shape
    result = accum / total[:, :, None]
    return jnp.transpose(result, (1, 0, 2)).reshape(rows, heads * head_size).astype(jnp.bfloat16)


def per_device(
    clean,
    noise,
    noise_two,
    steps_gen,
    steps_teacher,
    cache_key,
    cache_value,
    cache_block,
    span_block,
    gen_query,
    gen_key,
    gen_value,
    gen_out,
    teacher_query,
    teacher_key,
    teacher_value,
    teacher_out,
):
    ctx_count = lax.axis_size("ctx")
    fsdp_count = lax.axis_size("fsdp")
    tok_dev = clean.shape[0]
    block_rows = tok_dev * fsdp_count
    total = block_rows * ctx_count
    offset = (lax.axis_index("ctx") * fsdp_count + lax.axis_index("fsdp")) * tok_dev
    width = gen_query.shape[1]
    heads = width // HEAD
    sig_gen = sigmas(steps_gen, offset, tok_dev, total)
    mixed = (
        (1.0 - sig_gen) * clean.astype(jnp.float32) + sig_gen * noise.astype(jnp.float32)
    ).astype(jnp.bfloat16)
    gen_stack = jnp.concatenate([gen_query, gen_key, gen_value], axis=1)
    projected = jnp.dot(
        normed(lax.all_gather(mixed, "fsdp", axis=0, tiled=True)),
        gen_stack,
        preferred_element_type=jnp.float32,
    ).astype(jnp.bfloat16)
    query = projected[:, :width]
    key = projected[:, width : 2 * width]
    value = projected[:, 2 * width :]
    query_heads = query.reshape(block_rows, heads, HEAD)
    visible_cache = (cache_block < span_block[0]).astype(jnp.int32)
    start_state = empty_state(heads, block_rows, HEAD)
    keys_all = jnp.concatenate([cache_key, key], axis=0)
    values_all = jnp.concatenate([cache_value, value], axis=0)
    flags = jnp.concatenate([visible_cache, jnp.ones((block_rows,), jnp.int32)])
    pieces = (
        lax.all_gather(keys_all, "ctx", axis=0, tiled=True),
        lax.all_gather(values_all, "ctx", axis=0, tiled=True),
        lax.all_gather(flags, "ctx", axis=0, tiled=True),
    )
    state = absorb(start_state, query_heads, pieces[0], pieces[1], pieces[2])
    attn = finish(state)
    gen_sum = lax.psum_scatter(
        jnp.dot(attn, gen_out, preferred_element_type=jnp.float32).astype(jnp.bfloat16),
        "fsdp",
        scatter_dimension=0,
        tiled=True,
    ).astype(jnp.float32)
    generated = (mixed.astype(jnp.float32) + gen_sum).astype(jnp.bfloat16)
    sig_teacher = sigmas(steps_teacher, offset, tok_dev, total)
    noisy = (
        (1.0 - sig_teacher) * generated.astype(jnp.float32)
        + sig_teacher * noise_two.astype(jnp.float32)
    ).astype(jnp.bfloat16)
    teacher_stack = jnp.concatenate([teacher_query, teacher_key, teacher_value], axis=1)
    teacher_proj = jnp.dot(
        normed(lax.all_gather(noisy, "fsdp", axis=0, tiled=True)),
        teacher_stack,
        preferred_element_type=jnp.float32,
    ).astype(jnp.bfloat16)
    teacher_heads = teacher_proj[:, :width].reshape(block_rows, heads, HEAD)
    t_key = teacher_proj[:, width : 2 * width]
    t_value = teacher_proj[:, 2 * width :]
    pieces = (
        lax.all_gather(t_key, "ctx", axis=0, tiled=True),
        lax.all_gather(t_value, "ctx", axis=0, tiled=True),
    )
    teacher_state = absorb(
        empty_state(heads, block_rows, HEAD), teacher_heads, pieces[0], pieces[1], None
    )
    teacher_attn = finish(teacher_state)
    teacher_sum = lax.psum_scatter(
        jnp.dot(teacher_attn, teacher_out, preferred_element_type=jnp.float32).astype(jnp.bfloat16),
        "fsdp",
        scatter_dimension=0,
        tiled=True,
    ).astype(jnp.float32)
    real = noisy.astype(jnp.float32) + teacher_sum
    cotangent = (generated.astype(jnp.float32) - real).astype(jnp.bfloat16)
    partial_grad = lax.dot_general(
        attn,
        lax.all_gather(cotangent, "fsdp", axis=0, tiled=True),
        (((0,), (0,)), ((), ())),
        preferred_element_type=jnp.float32,
    )
    grad_out = lax.psum(partial_grad.astype(jnp.bfloat16), "ctx")
    return (generated, grad_out)


def solution(mesh):
    in_specs = (
        P(("ctx", "fsdp"), None),
        P(("ctx", "fsdp"), None),
        P(("ctx", "fsdp"), None),
        P(),
        P(),
        P("ctx", "fsdp"),
        P("ctx", "fsdp"),
        P("ctx"),
        P(),
        P(None, "fsdp"),
        P(None, "fsdp"),
        P(None, "fsdp"),
        P("fsdp", None),
        P(None, "fsdp"),
        P(None, "fsdp"),
        P(None, "fsdp"),
        P("fsdp", None),
    )
    out_specs = (P(("ctx", "fsdp"), None), P("fsdp", None))
    return jax.shard_map(
        per_device, mesh=mesh, in_specs=in_specs, out_specs=out_specs, check_vma=False
    )
```

profile of v0, /device:TPU:0, one launch (start us, length us, event | category | flops | bytes accessed | tf_op | source)
XLA Modules:
  0.0 596.6 jit_solution(12653815185087535722)
XLA Ops:
  7.2 0.7 add_divide_fusion
  7.9 0.1 select_reduce_fusion
  8.0 2.0 add_convert_fusion.1
  10.0 0.0 all-gather.11.cloned.1.call-start
  10.1 33.2 %all-gather.9.cloned.1.call-done = bf16[256,5120]{1,0:T(8,128)(2,1)} async-done(((bf16[32,5120]{1,0:T(8,128)(2,1)}), bf16[256,5120]{1,0:T(8,128)(2,1)}) %all-gather.9.cloned.1.call-update) | async-done | bytes 2621456 | tf_op jit(solution)/shard_map/all_gather | solution.py:107
  43.3 2.3 fusion.15
  45.7 8.7 %fusion.33 = bf16[256,1536]{1,0:T(8,128)(2,1)S(1)} fusion(bf16[5120,512]{1,0:T(8,128)(2,1)} %param.28, bf16[5120,512]{1,0:T(8,128)(2,1)} %param.27, bf16[5120,512]{1,0:T(8,128)(2,1)} %param.26, bf16[256,5120]{1,0:T(8,128)(2,1)} %all-gather.9.cloned.1.call-done, f32[256]{0:T(256)S(1)} %add_rsqrt_fusion.1), kind=kOutput, calls=%fused_computation.37 | convolution fusion | flops 4078043136 | bytes 19137536 | tf_op jit(solution)/shard_map/dot_general | solution.py:106
  54.4 0.1 slice_bitcast_fusion.1
  54.5 0.8 pad_maximum_fusion
  55.3 0.0 all-gather.13.cloned.1.call-start
  55.4 0.8 pad_maximum_fusion.1
  56.2 0.0 reduce-scatter.3.cloned.1.call-start
  57.0 12.0 %all-gather = s32[4,1,512]{2,1,0:T(1,128)S(1)} all-gather(s32[1,1,512]{2,1,0:T(1,128)S(1)} %bitcast.73), channel_id=1, replica_groups=mesh['ctx'=4,'fsdp'=8] {'ctx'}, dimensions={0}, use_global_device_ids=true | all-gather | bytes 10240 | tf_op jit(solution)/shard_map/all_gather | solution.py:123
  69.0 32.4 %all-gather.11.cloned.1.call-done = bf16[2048,512]{1,0:T(8,128)(2,1)} async-done(((bf16[512,512]{1,0:T(8,128)(2,1)}), bf16[2048,512]{1,0:T(8,128)(2,1)}) %all-gather.11.cloned.1.call-update) | async-done | bytes 2097168 | tf_op jit(solution)/shard_map/all_gather | solution.py:121
  101.4 3.1 fusion.12
  104.6 3.2 copy-done
  107.8 2.2 fusion.13
  110.0 38.3 %all-gather.13.cloned.1.call-done = bf16[2048,512]{1,0:T(8,128)(2,1)} async-done(((bf16[512,512]{1,0:T(8,128)(2,1)}), bf16[2048,512]{1,0:T(8,128)(2,1)}) %all-gather.13.cloned.1.call-update) | async-done | bytes 2097168 | tf_op jit(solution)/shard_map/all_gather | solution.py:122
  148.3 3.0 copy.43
  151.3 5.5 fusion.63
  156.8 3.0 convolution_convert_fusion.2
  159.9 0.0 all-gather.15.cloned.1.call-start
  160.0 42.5 %reduce-scatter.3.cloned.1.call-done = bf16[32,5120]{1,0:T(8,128)(2,1)} async-done(((bf16[256,5120]{1,0:T(8,128)(2,1)}), bf16[32,5120]{1,0:T(8,128)(2,1)}) %reduce-scatter.3.cloned.1.call-update) | async-done | bytes 327696 | tf_op jit(solution)/shard_map/reduce_scatter | solution.py:127
  202.5 1.9 fusion.67
  204.4 0.2 all-gather.17.cloned.1.call-start
  204.6 30.0 %all-gather.15.cloned.1.call-done = bf16[256,5120]{1,0:T(8,128)(2,1)} async-done(((bf16[32,5120]{1,0:T(8,128)(2,1)}), bf16[256,5120]{1,0:T(8,128)(2,1)}) %all-gather.15.cloned.1.call-update) | async-done | bytes 2621456 | tf_op jit(solution)/shard_map/all_gather | solution.py:141
  234.6 2.3 fusion.17
  237.0 8.7 %fusion.28 = bf16[256,1536]{1,0:T(8,128)(2,1)S(1)} fusion(bf16[5120,512]{1,0:T(8,128)(2,1)} %param.32, bf16[5120,512]{1,0:T(8,128)(2,1)} %param.31, bf16[5120,512]{1,0:T(8,128)(2,1)} %param.30, bf16[256,5120]{1,0:T(8,128)(2,1)} %all-gather.15.cloned.1.call-done, f32[256]{0:T(256)S(1)} %add_rsqrt_fusion), kind=kOutput, calls=%fused_computation.36 | convolution fusion | flops 4078043136 | bytes 19137536 | tf_op jit(solution)/shard_map/dot_general | solution.py:140
  245.6 0.8 slice_bitcast_fusion
  246.5 0.0 all-gather.19.cloned.1.call-start
  246.6 0.7 all-gather.19.cloned.1.call-update
  247.3 0.0 reduce-scatter.5.cloned.1.call-start
  247.3 27.3 %all-gather.17.cloned.1.call-done = bf16[1024,512]{1,0:T(8,128)(2,1)} async-done(((bf16[256,512]{1,0:T(8,128)(2,1)}), bf16[1024,512]{1,0:T(8,128)(2,1)}) %all-gather.17.cloned.1.call-update) | async-done | bytes 1048592 | tf_op jit(solution)/shard_map/all_gather | solution.py:149
  274.6 2.0 multiply_reduce_fusion
  276.6 2.0 copy-done.1
  278.6 0.9 fusion.22
  279.6 24.1 %all-gather.19.cloned.1.call-done = bf16[1024,512]{1,0:T(8,128)(2,1)} async-done(((bf16[256,512]{1,0:T(8,128)(2,1)}), bf16[1024,512]{1,0:T(8,128)(2,1)}) %all-gather.19.cloned.1.call-update) | async-done | bytes 1048592 | tf_op jit(solution)/shard_map/all_gather | solution.py:150
  303.6 1.5 copy.44
  305.1 3.2 fusion.54
  308.3 5.6 convolution_convert_fusion.1
  313.9 0.0 all-gather.21.cloned.1.call-start
  314.0 43.3 %reduce-scatter.5.cloned.1.call-done = bf16[32,5120]{1,0:T(8,128)(2,1)} async-done(((bf16[256,5120]{1,0:T(8,128)(2,1)}), bf16[32,5120]{1,0:T(8,128)(2,1)}) %reduce-scatter.5.cloned.1.call-update) | async-done | bytes 327696 | tf_op jit(solution)/shard_map/reduce_scatter | solution.py:156
  357.2 1.8 fusion.68
  359.1 0.0 all-reduce.3.cloned.1.call-start
  359.1 30.7 %all-gather.21.cloned.1.call-done = bf16[256,5120]{1,0:T(8,128)(2,1)} async-done(((bf16[32,5120]{1,0:T(8,128)(2,1)}), bf16[256,5120]{1,0:T(8,128)(2,1)}) %all-gather.21.cloned.1.call-update) | async-done | bytes 2621456 | tf_op jit(solution)/shard_map/all_gather | solution.py:166
  389.8 5.6 convolution_convert_fusion
  395.5 189.1 %all-reduce.3.cloned.1.call-done = bf16[512,5120]{1,0:T(8,128)(2,1)} async-done(((bf16[512,5120]{1,0:T(8,128)(2,1)}), bf16[512,5120]{1,0:T(8,128)(2,1)}) %all-reduce.3.cloned.1.call-update) | async-done | bytes 5242896 | tf_op jit(solution)/shard_map/psum | solution.py:170
  584.6 5.2 copy.76
  (42 shorter events, 0.3 us)
Async XLA Ops:
  7.2 36.1 %all-gather.9.cloned.1.call-start = ((), (), s32[]{:S(2)}) async-start(), calls=%async_computation.2 | async-start | bytes 2949120 | tf_op jit(solution)/shard_map/all_gather | solution.py:107
  10.0 91.4 %all-gather.11.cloned.1.call-start = ((), (), s32[]{:S(2)}) async-start(), calls=%async_computation.3 | async-start | bytes 2621440 | tf_op jit(solution)/shard_map/all_gather | solution.py:121
  45.7 8.8 %copy-start.6 = (bf16[256,512]{1,0:T(8,128)(2,1)S(1)}, bf16[256,512]{1,0:T(8,128)(2,1)}, u32[]{:S(2)}) copy-start(bf16[256,512]{1,0:T(8,128)(2,1)} %param.22) | copy-start | bytes 786436
  45.7 9.7 %copy-start.7 = (bf16[256,512]{1,0:T(8,128)(2,1)S(1)}, bf16[256,512]{1,0:T(8,128)(2,1)}, u32[]{:S(2)}) copy-start(bf16[256,512]{1,0:T(8,128)(2,1)} %param.23) | copy-start | bytes 786436
  45.7 11.3 %copy-start.8 = (s32[256]{0:T(256)S(1)}, s32[256]{0:T(256)}, u32[]{:S(2)}) copy-start(s32[256]{0:T(256)} %param.24) | copy-start | bytes 3076
  55.3 93.0 %all-gather.13.cloned.1.call-start = ((), (), s32[]{:S(2)}) async-start(), calls=%async_computation.4 | async-start | bytes 2621440 | tf_op jit(solution)/shard_map/all_gather | solution.py:122
  56.2 146.2 %reduce-scatter.3.cloned.1.call-start = ((), (), s32[]{:S(2)}) async-start(), calls=%async_computation.5 | async-start | bytes 2949120 | tf_op jit(solution)/shard_map/reduce_scatter | solution.py:127
  104.5 3.2 copy-start
  148.3 8.5 %slice-start = ((s8[5242880]{0:T(1024)(128)(4,1)}), s8[1048576]{0:T(1024)(128)(4,1)S(1)}, s32[]{:S(2)}) async-start(s8[5242880]{0:T(1024)(128)(4,1)} %bitcast.63), calls=%async_computation.12 | async-start | bytes 2097152
  151.3 5.5 slice-start.1
  156.8 45.6 %copy-start.3 = (bf16[32,5120]{1,0:T(8,128)(2,1)S(1)}, bf16[32,5120]{1,0:T(8,128)(2,1)}, u32[]{:S(2)}) copy-start(bf16[32,5120]{1,0:T(8,128)(2,1)} %add_convert_fusion.1) | copy-start | bytes 983044
  156.8 45.6 %copy-start.5 = (bf16[32,5120]{1,0:T(8,128)(2,1)S(1)}, bf16[32,5120]{1,0:T(8,128)(2,1)}, u32[]{:S(2)}) copy-start(bf16[32,5120]{1,0:T(8,128)(2,1)} %param.19) | copy-start | bytes 983044
  159.9 74.7 %all-gather.15.cloned.1.call-start = ((), (), s32[]{:S(2)}) async-start(), calls=%async_computation.6 | async-start | bytes 2949120 | tf_op jit(solution)/shard_map/all_gather | solution.py:141
  204.4 152.9 %copy-start.4 = (bf16[32,5120]{1,0:T(8,128)(2,1)}, bf16[32,5120]{1,0:T(8,128)(2,1)S(1)}, u32[]{:S(2)}) copy-start(bf16[32,5120]{1,0:T(8,128)(2,1)S(1)} %get-tuple-element.18) | copy-start | bytes 983044
  204.4 70.2 %all-gather.17.cloned.1.call-start = ((), (), s32[]{:S(2)}) async-start(), calls=%async_computation.7 | async-start | bytes 1310720 | tf_op jit(solution)/shard_map/all_gather | solution.py:149
  246.5 57.1 %all-gather.19.cloned.1.call-start = ((), (), s32[]{:S(2)}) async-start(), calls=%async_computation.8 | async-start | bytes 1310720 | tf_op jit(solution)/shard_map/all_gather | solution.py:150
  247.3 110.0 %reduce-scatter.5.cloned.1.call-start = ((), (), s32[]{:S(2)}) async-start(), calls=%async_computation.9 | async-start | bytes 2949120 | tf_op jit(solution)/shard_map/reduce_scatter | solution.py:156
  276.6 2.0 copy-start.1
  308.3 48.9 %copy-start.2 = (bf16[32,5120]{1,0:T(8,128)(2,1)S(1)}, bf16[32,5120]{1,0:T(8,128)(2,1)}, u32[]{:S(2)}) copy-start(bf16[32,5120]{1,0:T(8,128)(2,1)} %get-tuple-element.4) | copy-start | bytes 983044
  313.9 75.9 %all-gather.21.cloned.1.call-start = ((), (), s32[]{:S(2)}) async-start(), calls=%async_computation.10 | async-start | bytes 2949120 | tf_op jit(solution)/shard_map/all_gather | solution.py:166
  359.1 225.5 %all-reduce.3.cloned.1.call-start = ((), (), s32[]{:S(2)}) async-start(), calls=%async_computation.11 | async-start | bytes 10485760 | tf_op jit(solution)/shard_map/psum | solution.py:170
Sparse Core Ops, SparseCore 0:
  10.5 32.8 all-gather.8
  55.4 45.9 all-gather.10
  103.6 44.6 all-gather.12
  160.0 42.3 reduce-scatter.2
  204.5 30.0 all-gather.14
  246.6 27.9 all-gather.16
  276.2 27.4 all-gather.18
  314.1 43.1 reduce-scatter.4
  359.7 30.0 all-gather.20
  395.6 188.9 all-reduce.2
where the time goes:
time: 597 us
  waiting for transfers between devices  492 us (82%)
  matrix products  45.4 us (8%)
  other arithmetic  16 us (3%)
  local copies, waits for them, and re-layouts  15.8 us (3%)
  between operations  15.1 us (3%)
  blocking collectives  12 us (2%)
    psum x1, waiting for transfers between devices, per_device(): grad_out = lax.psum(partial_grad.astype(jnp.bfloat16), 'ctx')  189 us
    reduce_scatter x1, waiting for transfers between devices, per_device(): lax.psum_scatter(jnp.dot(teacher_attn, teacher_out, preferred_element_typ...  43.3 us
    reduce_scatter x1, waiting for transfers between devices, per_device(): lax.psum_scatter(jnp.dot(attn, gen_out, preferred_element_type=jnp.float3...  42.5 us
    all_gather x1, waiting for transfers between devices, per_device(): lax.all_gather(values_all, 'ctx', axis=0, tiled=True)  38.3 us
    all_gather x1, waiting for transfers between devices, per_device(): lax.all_gather(mixed, 'fsdp', axis=0, tiled=True)  33.2 us
    all_gather x1, waiting for transfers between devices, per_device(): lax.all_gather(keys_all, 'ctx', axis=0, tiled=True)  32.4 us
    all_gather x1, waiting for transfers between devices, per_device(): lax.all_gather(cotangent, 'fsdp', axis=0, tiled=True)  30.7 us
    all_gather x1, waiting for transfers between devices, per_device(): lax.all_gather(noisy, 'fsdp', axis=0, tiled=True)  30 us
  transfers between devices with their start and end apart: 10, of which 10 were waited for; matrix products, arithmetic and copies ran while one was open for 2% of the time, Pallas kernels for 0%

commit v1 on v0

v1 whole, which is shorter than its diff:
```python
import jax
import jax.numpy as jnp
from jax import lax
from jax.sharding import PartitionSpec as P

HEAD = 128
FRAMES = 3
STEPS = 1000


SHIFT = 5.0
EPS = 1e-06


def sigmas(steps, offset, count, total):
    level = 1.0 - steps.astype(jnp.float32) / STEPS
    sig = SHIFT * level / (1.0 + (SHIFT - 1.0) * level)
    positions = offset + jnp.arange(count, dtype=jnp.int32)
    frame = positions * FRAMES // total
    match = (frame[:, None] == jnp.arange(FRAMES, dtype=jnp.int32)[None, :]).astype(jnp.float32)
    return jnp.sum(match * sig[None, :], axis=1)[:, None]


def normed(values):
    wide = values.astype(jnp.float32)
    return (wide * lax.rsqrt(jnp.mean(wide * wide, axis=1, keepdims=True) + EPS)).astype(
        jnp.bfloat16
    )


def attend(query_heads, parts):
    head_size = query_heads.shape[2]
    scale = 1.0 / head_size**0.5
    all_scores = []
    for keys, _, allowed in parts:
        scores = (
            jnp.einsum("rhd,phd->hrp", query_heads, keys, preferred_element_type=jnp.float32)
            * scale
        )
        if allowed is not None:
            scores = jnp.where(allowed[None, None, :], scores, -1e30)
        all_scores.append(scores)
    top = all_scores[0].max(axis=2)
    for scores in all_scores[1:]:
        top = jnp.maximum(top, scores.max(axis=2))
    total = 0.0
    accum = 0.0
    for scores, (_, values, allowed) in zip(all_scores, parts):
        weights = jnp.exp(scores - top[:, :, None])
        if allowed is not None:
            weights = jnp.where(allowed[None, None, :], weights, 0.0)
        total = total + weights.sum(axis=2)
        accum = accum + jnp.einsum(
            "hrp,phd->hrd",
            weights.astype(jnp.bfloat16),
            values,
            preferred_element_type=jnp.float32,
        )
    heads, rows, _ = accum.shape
    result = accum / total[:, :, None]
    return jnp.transpose(result, (1, 0, 2)).reshape(rows, heads * head_size).astype(jnp.bfloat16)


def per_device(
    clean,
    noise,
    noise_two,
    steps_gen,
    steps_teacher,
    cache_key,
    cache_value,
    cache_block,
    span_block,
    gen_query,
    gen_key,
    gen_value,
    gen_out,
    teacher_query,
    teacher_key,
    teacher_value,
    teacher_out,
):
    ctx_count = lax.axis_size("ctx")
    fsdp_count = lax.axis_size("fsdp")
    tok_dev = clean.shape[0]
    block_rows = tok_dev * fsdp_count
    total = block_rows * ctx_count
    offset = (lax.axis_index("ctx") * fsdp_count + lax.axis_index("fsdp")) * tok_dev
    width = gen_query.shape[1]
    heads = width // HEAD
    sig_gen = sigmas(steps_gen, offset, tok_dev, total)
    mixed = (
        (1.0 - sig_gen) * clean.astype(jnp.float32) + sig_gen * noise.astype(jnp.float32)
    ).astype(jnp.bfloat16)
    slots = cache_block.shape[0]
    visible = (cache_block < span_block[0]).astype(jnp.bfloat16)
    flag_rows = -(-slots // (16 * width)) * 16
    flags = jnp.pad(visible, (0, flag_rows * width - slots)).reshape(flag_rows, width)
    cache = lax.all_gather(
        jnp.concatenate([cache_key, cache_value, flags], axis=0), "ctx", axis=0, tiled=False
    )
    gen_stack = jnp.concatenate([gen_query, gen_key, gen_value], axis=1)
    projected = jnp.dot(
        normed(lax.all_gather(mixed, "fsdp", axis=0, tiled=True)),
        gen_stack,
        preferred_element_type=jnp.float32,
    ).astype(jnp.bfloat16)
    query_heads = projected[:, :width].reshape(block_rows, heads, HEAD)
    span = lax.all_gather(projected[:, width:], "ctx", axis=0, tiled=True)
    slots_all = slots * ctx_count
    cached_keys = cache[:, :slots].reshape(slots_all, heads, HEAD)
    cached_values = cache[:, slots : 2 * slots].reshape(slots_all, heads, HEAD)
    allowed = cache[:, 2 * slots :].reshape(ctx_count, -1)[:, :slots].reshape(-1) > 0
    attn = attend(
        query_heads,
        (
            (cached_keys, cached_values, allowed),
            (
                span[:, :width].reshape(total, heads, HEAD),
                span[:, width:].reshape(total, heads, HEAD),
                None,
            ),
        ),
    )
    attn_all = lax.all_gather(attn, "ctx", axis=0, tiled=True)
    gen_sum = lax.psum_scatter(
        jnp.dot(attn, gen_out, preferred_element_type=jnp.float32).astype(jnp.bfloat16),
        "fsdp",
        scatter_dimension=0,
        tiled=True,
    ).astype(jnp.float32)
    generated = (mixed.astype(jnp.float32) + gen_sum).astype(jnp.bfloat16)
    sig_teacher = sigmas(steps_teacher, offset, tok_dev, total)
    noisy = (
        (1.0 - sig_teacher) * generated.astype(jnp.float32)
        + sig_teacher * noise_two.astype(jnp.float32)
    ).astype(jnp.bfloat16)
    teacher_stack = jnp.concatenate([teacher_query, teacher_key, teacher_value], axis=1)
    teacher_proj = jnp.dot(
        normed(lax.all_gather(noisy, "fsdp", axis=0, tiled=True)),
        teacher_stack,
        preferred_element_type=jnp.float32,
    ).astype(jnp.bfloat16)
    teacher_heads = teacher_proj[:, :width].reshape(block_rows, heads, HEAD)
    t_span = lax.all_gather(teacher_proj[:, width:], "ctx", axis=0, tiled=True)
    teacher_attn = attend(
        teacher_heads,
        (
            (
                t_span[:, :width].reshape(total, heads, HEAD),
                t_span[:, width:].reshape(total, heads, HEAD),
                None,
            ),
        ),
    )
    teacher_sum = lax.psum_scatter(
        jnp.dot(teacher_attn, teacher_out, preferred_element_type=jnp.float32).astype(jnp.bfloat16),
        "fsdp",
        scatter_dimension=0,
        tiled=True,
    ).astype(jnp.float32)
    real = noisy.astype(jnp.float32) + teacher_sum
    cotangent = (generated.astype(jnp.float32) - real).astype(jnp.bfloat16)
    grad_out = lax.dot_general(
        attn_all,
        lax.all_gather(cotangent, ("ctx", "fsdp"), axis=0, tiled=True),
        (((0,), (0,)), ((), ())),
        preferred_element_type=jnp.float32,
    ).astype(jnp.bfloat16)
    return (generated, grad_out)


def solution(mesh):
    in_specs = (
        P(("ctx", "fsdp"), None),
        P(("ctx", "fsdp"), None),
        P(("ctx", "fsdp"), None),
        P(),
        P(),
        P("ctx", "fsdp"),
        P("ctx", "fsdp"),
        P("ctx"),
        P(),
        P(None, "fsdp"),
        P(None, "fsdp"),
        P(None, "fsdp"),
        P("fsdp", None),
        P(None, "fsdp"),
        P(None, "fsdp"),
        P(None, "fsdp"),
        P("fsdp", None),
    )
    out_specs = (P(("ctx", "fsdp"), None), P("fsdp", None))
    return jax.shard_map(
        per_device, mesh=mesh, in_specs=in_specs, out_specs=out_specs, check_vma=False
    )
```

time: 597 us -> 477 us (0.80)
  waiting for transfers between devices: 492 us -> 386 us
  blocking collectives: 12 us -> 0 us
    psum x1 -> x0, waiting for transfers between devices: 189 us -> none  [per_device(): grad_out = lax.psum(partial_grad.astype(jnp.bfloat16), 'ctx')]
    all_gather x5, waiting for transfers between devices: 153 us -> 241 us  [the longest x1 88.5 us: per_device(): lax.all_gather(cotangent, ('ctx', 'fsdp'), axis=0, tiled=True)]
    all_gather x1 -> x0, blocking collectives: 12 us -> none  [per_device(): lax.all_gather(flags, 'ctx', axis=0, tiled=True)]
    unnamed x26 -> x25, local copies, waits for them, and re-layouts: 11.4 us -> 5.27 us
    dot_general x5 -> x7, matrix products: 19.4 us -> 18.8 us  [the longest x1 10 us: per_device(): lax.dot_general(attn_all, lax.all_gather(cotangent, ('ctx', 'fsdp'), axis...]
  transfers between devices with their start and end apart: 10 -> 9, of which waited for: 10 -> 9; matrix products, arithmetic and copies ran while one was open for 2% -> 5% of each run, Pallas kernels for 0% -> 0%
where the time goes in v1:
time: 477 us
  waiting for transfers between devices  386 us (81%)
  matrix products  44.9 us (9%)
  other arithmetic  16.6 us (3%)
  between operations  14.7 us (3%)
  local copies, waits for them, and re-layouts  13.8 us (3%)
    all_gather x1, waiting for transfers between devices, per_device(): lax.all_gather(cotangent, ('ctx', 'fsdp'), axis=0, tiled=True)  88.5 us
    all_gather x1, waiting for transfers between devices, per_device(): t_span = lax.all_gather(teacher_proj[:, width:], 'ctx', axis=0, tiled=True)  46.1 us
    reduce_scatter x1, waiting for transfers between devices, per_device(): lax.psum_scatter(jnp.dot(attn, gen_out, preferred_element_type=jnp.float3...  42.5 us
    reduce_scatter x1, waiting for transfers between devices, per_device(): lax.psum_scatter(jnp.dot(teacher_attn, teacher_out, preferred_element_typ...  41.8 us
    all_gather x1, waiting for transfers between devices, per_device(): span = lax.all_gather(projected[:, width:], 'ctx', axis=0, tiled=True)  39.3 us
    all_gather x1, waiting for transfers between devices, per_device(): lax.all_gather(jnp.concatenate([cache_key, cache_value, flags], axis=0),...  37.4 us
    all_gather x1, waiting for transfers between devices, per_device(): lax.all_gather(noisy, 'fsdp', axis=0, tiled=True)  30 us
    all_gather x1, waiting for transfers between devices, per_device(): lax.all_gather(mixed, 'fsdp', axis=0, tiled=True)  29.9 us
  transfers between devices with their start and end apart: 9, of which 9 were waited for; matrix products, arithmetic and copies ran while one was open for 5% of the time, Pallas kernels for 0%

profile of v1, /device:TPU:0, one launch (start us, length us, event | category | flops | bytes accessed | tf_op | source)
XLA Modules:
  0.0 476.9 jit_solution(1163997069562912004)
XLA Ops:
  7.2 0.7 add_divide_fusion
  7.9 0.1 select_reduce_fusion
  8.0 2.0 add_convert_fusion.1
  10.7 0.7 broadcast_compare_fusion
  11.4 1.9 pad_maximum_fusion
  13.4 29.9 %all-gather.9.cloned.1.call-done = bf16[256,5120]{1,0:T(8,128)(2,1)} async-done(((bf16[32,5120]{1,0:T(8,128)(2,1)}), bf16[256,5120]{1,0:T(8,128)(2,1)}) %all-gather.9.cloned.1.call-update) | async-done | bytes 2621456 | tf_op jit(solution)/shard_map/all_gather | solution.py:104
  43.3 2.3 fusion.12
  45.7 8.7 %fusion.32 = bf16[256,1536]{1,0:T(8,128)(2,1)S(1)} fusion(bf16[5120,512]{1,0:T(8,128)(2,1)} %param.28, bf16[5120,512]{1,0:T(8,128)(2,1)} %param.27, bf16[5120,512]{1,0:T(8,128)(2,1)} %param.26, bf16[256,5120]{1,0:T(8,128)(2,1)} %all-gather.9.cloned.1.call-done, f32[256]{0:T(256)S(1)} %add_rsqrt_fusion.1), kind=kOutput, calls=%fused_computation.39 | convolution fusion | flops 4078043136 | bytes 19137536 | tf_op jit(solution)/shard_map/dot_general | solution.py:103
  54.3 0.9 slice.52
  55.3 37.4 %all-gather.21.cloned.1.call-done = bf16[2112,512]{1,0:T(8,128)(2,1)} async-done(((bf16[528,512]{1,0:T(8,128)(2,1)}), bf16[2112,512]{1,0:T(8,128)(2,1)}) %all-gather.21.cloned.1.call-update) | async-done | bytes 2162704 | tf_op jit(solution)/shard_map/all_gather | solution.py:99
  92.7 1.8 fusion.94
  94.5 1.1 reshape.123
  95.6 0.8 slice_bitcast_fusion.4
  96.5 0.1 copy.52
  96.6 0.3 reshape.113
  96.9 2.8 fusion.16
  99.7 39.3 %all-gather.11.cloned.1.call-done = bf16[1024,1024]{1,0:T(8,128)(2,1)} async-done(((bf16[256,1024]{1,0:T(8,128)(2,1)}), bf16[1024,1024]{1,0:T(8,128)(2,1)}) %all-gather.11.cloned.1.call-update) | async-done | bytes 2097168 | tf_op jit(solution)/shard_map/all_gather | solution.py:109
  139.0 1.8 fusion.95
  140.8 1.3 copy.46
  142.1 0.8 multiply_reduce_fusion.1
  142.9 1.4 copy-done
  144.3 0.3 copy-done.5
  144.6 1.2 fusion.45
  145.8 1.9 fusion.17
  147.7 1.0 fusion.75
  148.8 5.6 %convolution_convert_fusion.2 = bf16[256,5120]{1,0:T(8,128)(2,1)} fusion(bf16[256,512]{0,1:T(8,128)(2,1)S(1)} %bitcast.75, bf16[512,5120]{1,0:T(8,128)(2,1)} %param.29), kind=kOutput, calls=%fused_computation.18 | convolution fusion | flops 1343488000 | bytes 8126464 | tf_op jit(solution)/shard_map/dot_general | solution.py:127
  154.5 0.0 all-gather.15.cloned.1.call-start
  154.5 42.5 %reduce-scatter.3.cloned.1.call-done = bf16[32,5120]{1,0:T(8,128)(2,1)} async-done(((bf16[256,5120]{1,0:T(8,128)(2,1)}), bf16[32,5120]{1,0:T(8,128)(2,1)}) %reduce-scatter.3.cloned.1.call-update) | async-done | bytes 327696 | tf_op jit(solution)/shard_map/reduce_scatter | solution.py:126
  197.0 1.9 fusion.79
  198.9 0.2 all-gather.17.cloned.1.call-start
  199.2 30.0 %all-gather.15.cloned.1.call-done = bf16[256,5120]{1,0:T(8,128)(2,1)} async-done(((bf16[32,5120]{1,0:T(8,128)(2,1)}), bf16[256,5120]{1,0:T(8,128)(2,1)}) %all-gather.15.cloned.1.call-update) | async-done | bytes 2621456 | tf_op jit(solution)/shard_map/all_gather | solution.py:140
  229.2 2.3 fusion.14
  231.5 8.7 %fusion.27 = bf16[256,1536]{1,0:T(8,128)(2,1)S(1)} fusion(bf16[5120,512]{1,0:T(8,128)(2,1)} %param.32, bf16[5120,512]{1,0:T(8,128)(2,1)} %param.31, bf16[5120,512]{1,0:T(8,128)(2,1)} %param.30, bf16[256,5120]{1,0:T(8,128)(2,1)} %all-gather.15.cloned.1.call-done, f32[256]{0:T(256)S(1)} %add_rsqrt_fusion), kind=kOutput, calls=%fused_computation.38 | convolution fusion | flops 4078043136 | bytes 19137536 | tf_op jit(solution)/shard_map/dot_general | solution.py:139
  240.2 0.9 copy-done.7
  241.1 0.9 slice.57
  242.0 46.1 %all-gather.17.cloned.1.call-done = bf16[1024,1024]{1,0:T(8,128)(2,1)} async-done(((bf16[256,1024]{1,0:T(8,128)(2,1)}), bf16[1024,1024]{1,0:T(8,128)(2,1)}) %all-gather.17.cloned.1.call-update) | async-done | bytes 2097168 | tf_op jit(solution)/shard_map/all_gather | solution.py:145
  288.1 1.8 slice_bitcast_fusion
  289.8 0.5 copy.47
  290.4 1.9 multiply_reduce_fusion
  292.3 0.9 fusion.19
  293.2 1.0 fusion.60
  294.3 3.1 convolution_convert_fusion.1
  297.5 0.7 all-gather.13.cloned.1.call-update
  298.2 41.8 %reduce-scatter.5.cloned.1.call-done = bf16[32,5120]{1,0:T(8,128)(2,1)} async-done(((bf16[256,5120]{1,0:T(8,128)(2,1)}), bf16[32,5120]{1,0:T(8,128)(2,1)}) %reduce-scatter.5.cloned.1.call-update) | async-done | bytes 327696 | tf_op jit(solution)/shard_map/reduce_scatter | solution.py:156
  340.0 1.8 fusion.80
  341.8 29.9 %all-gather.13.cloned.1.call-done = bf16[1024,512]{0,1:T(8,128)(2,1)} async-done(((bf16[256,512]{0,1:T(8,128)(2,1)}), bf16[1024,512]{0,1:T(8,128)(2,1)}) %all-gather.13.cloned.1.call-update) | async-done | bytes 1048592 | tf_op jit(solution)/shard_map/all_gather | solution.py:125
  371.8 88.5 %all-gather.19.cloned.1.call-done = bf16[1024,5120]{1,0:T(8,128)(2,1)} async-done(((bf16[32,5120]{1,0:T(8,128)(2,1)}), bf16[1024,5120]{1,0:T(8,128)(2,1)}) %all-gather.19.cloned.1.call-update) | async-done | bytes 10485776 | tf_op jit(solution)/shard_map/all_gather | solution.py:166
  460.3 10.0 %convolution_convert_fusion = bf16[512,5120]{1,0:T(8,128)(2,1)} fusion(bf16[1024,512]{0,1:T(8,128)(2,1)} %all-gather.13.cloned.1.call-done, bf16[1024,5120]{1,0:T(8,128)(2,1)} %all-gather.19.cloned.1.call-done), kind=kOutput, calls=%fused_computation.12 | convolution fusion | flops 5371330560 | bytes 16777216 | tf_op jit(solution)/shard_map/dot_general | solution.py:164
  (46 shorter events, 0.6 us)
Async XLA Ops:
  7.2 36.1 %all-gather.9.cloned.1.call-start = ((), (), s32[]{:S(2)}) async-start(), calls=%async_computation.2 | async-start | bytes 2949120 | tf_op jit(solution)/shard_map/all_gather | solution.py:104
  10.0 82.7 %all-gather.21.cloned.1.call-start = ((), (), s32[]{:S(2)}) async-start(), calls=%async_computation.10 | async-start | bytes 2703360 | tf_op jit(solution)/shard_map/all_gather | solution.py:99
  13.3 125.7 %all-gather.11.cloned.1.call-start = ((), (), s32[]{:S(2)}) async-start(), calls=%async_computation.3 | async-start | bytes 2621440 | tf_op jit(solution)/shard_map/all_gather | solution.py:109
  55.2 141.8 %reduce-scatter.3.cloned.1.call-start = ((), (), s32[]{:S(2)}) async-start(), calls=%async_computation.4 | async-start | bytes 2949120 | tf_op jit(solution)/shard_map/reduce_scatter | solution.py:126
  142.1 2.2 copy-start
  142.1 2.5 copy-start.5
  145.8 2.0 copy-start.6
  148.8 5.7 %copy-start.3 = (bf16[256,4,128]{0,2,1:T(8,128)(2,1)}, bf16[256,4,128]{0,2,1:T(8,128)(2,1)S(1)}, u32[]{:S(2)}) copy-start(bf16[256,4,128]{0,2,1:T(8,128)(2,1)S(1)} %fusion.75) | copy-start | bytes 786436
  148.8 48.2 %copy-start.2 = (bf16[32,5120]{1,0:T(8,128)(2,1)S(1)}, bf16[32,5120]{1,0:T(8,128)(2,1)}, u32[]{:S(2)}) copy-start(bf16[32,5120]{1,0:T(8,128)(2,1)} %add_convert_fusion.1) | copy-start | bytes 983044
  148.8 48.2 %copy-start.8 = (bf16[32,5120]{1,0:T(8,128)(2,1)S(1)}, bf16[32,5120]{1,0:T(8,128)(2,1)}, u32[]{:S(2)}) copy-start(bf16[32,5120]{1,0:T(8,128)(2,1)} %param.19) | copy-start | bytes 983044
  154.5 74.7 %all-gather.15.cloned.1.call-start = ((), (), s32[]{:S(2)}) async-start(), calls=%async_computation.6 | async-start | bytes 2949120 | tf_op jit(solution)/shard_map/all_gather | solution.py:140
  198.9 141.1 %copy-start.4 = (bf16[32,5120]{1,0:T(8,128)(2,1)}, bf16[32,5120]{1,0:T(8,128)(2,1)S(1)}, u32[]{:S(2)}) copy-start(bf16[32,5120]{1,0:T(8,128)(2,1)S(1)} %get-tuple-element.7) | copy-start | bytes 983044
  198.9 89.1 %all-gather.17.cloned.1.call-start = ((), (), s32[]{:S(2)}) async-start(), calls=%async_computation.7 | async-start | bytes 2621440 | tf_op jit(solution)/shard_map/all_gather | solution.py:145
  240.2 0.9 copy-start.7
  242.0 98.0 %reduce-scatter.5.cloned.1.call-start = ((), (), s32[]{:S(2)}) async-start(), calls=%async_computation.8 | async-start | bytes 2949120 | tf_op jit(solution)/shard_map/reduce_scatter | solution.py:156
  290.4 3.9 slice-start
  292.3 2.0 slice-start.1
  294.3 45.7 %copy-start.1 = (bf16[32,5120]{1,0:T(8,128)(2,1)S(1)}, bf16[32,5120]{1,0:T(8,128)(2,1)}, u32[]{:S(2)}) copy-start(bf16[32,5120]{1,0:T(8,128)(2,1)} %get-tuple-element.6) | copy-start | bytes 983044
  297.4 74.3 %all-gather.13.cloned.1.call-start = ((), (), s32[]{:S(2)}) async-start(), calls=%async_computation.5 | async-start | bytes 1310720 | tf_op jit(solution)/shard_map/all_gather | solution.py:125
  298.2 162.1 %all-gather.19.cloned.1.call-start = ((), (), s32[]{:S(2)}) async-start(), calls=%async_computation.9 | async-start | bytes 10813440 | tf_op jit(solution)/shard_map/all_gather | solution.py:166
Sparse Core Ops, SparseCore 0:
  10.5 32.8 all-gather.8
  45.4 47.2 all-gather.20
  94.3 44.6 all-gather.10
  154.6 42.3 reduce-scatter.2
  199.1 30.0 all-gather.14
  242.1 45.9 all-gather.16
  297.6 42.3 reduce-scatter.4
  341.6 30.1 all-gather.12
  375.2 85.0 all-gather.18

commit v2 on v1

--- a/solution.py
+++ b/solution.py
@@ -1,6 +1,10 @@
+import functools
+
 import jax
 import jax.numpy as jnp
 from jax import lax
+from jax.experimental import pallas as pl
+from jax.experimental.pallas import tpu as pltpu
 from jax.sharding import PartitionSpec as P
 
 HEAD = 128
@@ -59,6 +63,351 @@
     heads, rows, _ = accum.shape
     result = accum / total[:, :, None]
     return jnp.transpose(result, (1, 0, 2)).reshape(rows, heads * head_size).astype(jnp.bfloat16)
+
+
+MESH = pl.DeviceIdType.MESH
+VMEM_BYTES = 40 * 1024 * 1024
+
+
+class Place:
+    def __init__(self, ctx_count, fsdp_count):
+        self.ctx_count = ctx_count
+        self.count = fsdp_count
+        self.chips = fsdp_count // 2
+        self.z = lax.axis_index("ctx")
+        self.me = lax.axis_index("fsdp")
+        self.chip = lax.div(self.me, 2)
+        self.core = lax.rem(self.me, 2)
+        self.sibling = self.chip * 2 + 1 - self.core
+
+    def ahead(self, step):
+        return lax.rem(self.chip + step, self.chips) * 2
+
+    def behind(self, step):
+        return lax.rem(self.chip + self.chips - step, self.chips) * 2
+
+    def group_targets(self):
+        same_core = [(self.z, self.ahead(j) + self.core) for j in range(1, self.chips)]
+        return same_core + [(self.z, self.sibling)]
+
+    def ctx_ahead(self, step):
+        return lax.rem(self.z + step, self.ctx_count)
+
+    def ctx_behind(self, step):
+        return lax.rem(self.z + self.ctx_count - step, self.ctx_count)
+
+    def ctx_targets(self):
+        return [(self.ctx_ahead(i), self.me) for i in range(1, self.ctx_count)]
+
+
+def greet(targets):
+    barrier = pltpu.get_barrier_semaphore()
+    for target in targets:
+        pl.semaphore_signal(barrier, inc=1, device_id=target, device_id_type=MESH)
+    pl.semaphore_wait(barrier, len(targets))
+
+
+def remote(src, dst, send_sem, recv_sem, target):
+    return pltpu.make_async_remote_copy(
+        src_ref=src,
+        dst_ref=dst,
+        send_sem=send_sem,
+        recv_sem=recv_sem,
+        device_id=target,
+        device_id_type=MESH,
+    )
+
+
+class Spread:
+    def __init__(self, place, src, out, row, sems, index):
+        self.place, self.src, self.out, self.row = place, src, out, row
+        self.send, self.recv, self.relay_send, self.relay_recv = (s.at[index] for s in sems)
+        self.relays = []
+
+    def own(self, step):
+        p = self.place
+        target = (p.z, p.sibling if step == 0 else p.ahead(step) + p.core)
+        return remote(
+            self.src, self.out.at[self.row + p.me], self.send.at[step], self.recv.at[step], target
+        )
+
+    def arrival(self, step):
+        p = self.place
+        source = p.sibling if step == 0 else p.behind(step) + p.core
+        return remote(
+            self.src,
+            self.out.at[self.row + source],
+            self.send.at[step],
+            self.recv.at[step],
+            (p.z, p.sibling),
+        )
+
+    def relay(self, step, core):
+        p = self.place
+        block = self.out.at[self.row + p.behind(step) + core]
+        return remote(
+            block, block, self.relay_send.at[step], self.relay_recv.at[step], (p.z, p.sibling)
+        )
+
+    def start(self):
+        for step in list(range(1, self.place.chips)) + [0]:
+            self.own(step).start()
+
+    def forward(self):
+        for step in range(1, self.place.chips):
+            self.arrival(step).wait_recv()
+            self.relay(step, self.place.core).start()
+
+    def end(self):
+        p = self.place
+        self.arrival(0).wait_recv()
+        for step in range(1, p.chips):
+            self.relay(step, 1 - p.core).wait_recv()
+        for step in range(p.chips):
+            self.own(step).wait_send()
+        for step in range(1, p.chips):
+            self.relay(step, p.core).wait_send()
+
+
+def spread_sems(parts, chips):
+    return [pltpu.SemaphoreType.DMA((parts, chips)) for _ in range(4)]
+
+
+def group_kernel(ctx_count, fsdp_count, src, out, *sems):
+    place = Place(ctx_count, fsdp_count)
+    greet(place.group_targets())
+    spread = Spread(place, src, out, 0, sems[:4], 0)
+    spread.start()
+    local = pltpu.make_async_copy(src, out.at[place.me], sems[4])
+    local.start()
+    spread.forward()
+    spread.end()
+    local.wait()
+
+
+def group_gather(values, ctx_count, fsdp_count, identity):
+    rows, columns = values.shape
+    gathered = pl.pallas_call(
+        functools.partial(group_kernel, ctx_count, fsdp_count),
+        out_shape=jax.ShapeDtypeStruct((fsdp_count, rows, columns), values.dtype),
+        in_specs=[pl.BlockSpec(memory_space=pl.ANY)],
+        out_specs=pl.BlockSpec(memory_space=pl.ANY),
+        scratch_shapes=spread_sems(1, fsdp_count // 2) + [pltpu.SemaphoreType.DMA],
+        compiler_params=pltpu.CompilerParams(
+            collective_id=identity, has_side_effects=True, vmem_limit_bytes=VMEM_BYTES
+        ),
+    )(values)
+    return gathered.reshape(fsdp_count * rows, columns)
+
+
+def ctx_kernel(ctx_count, fsdp_count, src, out, send_sem, recv_sem, local_sem):
+    place = Place(ctx_count, fsdp_count)
+    greet(place.ctx_targets())
+
+    def copy(step, slot):
+        return remote(
+            src,
+            out.at[slot],
+            send_sem.at[step],
+            recv_sem.at[step],
+            (place.ctx_ahead(step), place.me),
+        )
+
+    for step in range(1, ctx_count):
+        copy(step, place.z).start()
+    local = pltpu.make_async_copy(src, out.at[place.z], local_sem)
+    local.start()
+    for step in range(1, ctx_count):
+        copy(step, place.ctx_behind(step)).wait_recv()
+    for step in range(1, ctx_count):
+        copy(step, place.z).wait_send()
+    local.wait()
+
+
+def ctx_gather(values, ctx_count, fsdp_count, identity):
+    rows, columns = values.shape
+    gathered = pl.pallas_call(
+        functools.partial(ctx_kernel, ctx_count, fsdp_count),
+        out_shape=jax.ShapeDtypeStruct((ctx_count, rows, columns), values.dtype),
+        in_specs=[pl.BlockSpec(memory_space=pl.ANY)],
+        out_specs=pl.BlockSpec(memory_space=pl.ANY),
+        scratch_shapes=[
+            pltpu.SemaphoreType.DMA((ctx_count,)),
+            pltpu.SemaphoreType.DMA((ctx_count,)),
+            pltpu.SemaphoreType.DMA,
+        ],
+        compiler_params=pltpu.CompilerParams(
+            collective_id=identity, has_side_effects=True, vmem_limit_bytes=VMEM_BYTES
+        ),
+    )(values)
+    return gathered.reshape(ctx_count * rows, columns)
+
+
+def scatter_sum(place, partial, pair, stage, inbox, sems):
+    pair_send, pair_recv, send, recv = sems
+    chips = place.chips
+
+    def swap(step):
+        return remote(
+            partial.at[place.ahead(step) + 1 - place.core],
+            pair.at[step],
+            pair_send.at[step],
+            pair_recv.at[step],
+            (place.z, place.sibling),
+        )
+
+    def give(step):
+        return remote(
+            stage.at[step],
+            inbox.at[step],
+            send.at[step],
+            recv.at[step],
+            (place.z, place.ahead(step) + place.core),
+        )
+
+    order = list(range(1, chips)) + [0]
+    for step in order:
+        swap(step).start()
+    for step in order:
+        swap(step).wait_recv()
+        if step > 0:
+            both = partial[place.ahead(step) + place.core].astype(jnp.float32) + pair[step].astype(
+                jnp.float32
+            )
+            stage[step] = both.astype(jnp.bfloat16)
+            give(step).start()
+    result = partial[place.me].astype(jnp.float32) + pair[0].astype(jnp.float32)
+    for step in range(1, chips):
+        give(step).wait_recv()
+        result = result + inbox[step].astype(jnp.float32)
+    for step in order:
+        swap(step).wait_send()
+        if step > 0:
+            give(step).wait_send()
+    return result
+
+
+def scatter_scratch(chips, rows, columns):
+    return [pltpu.VMEM((chips, rows, columns), jnp.bfloat16) for _ in range(3)] + [
+        pltpu.SemaphoreType.DMA((chips,)) for _ in range(4)
+    ]
+
+
+def renoise_kernel(
+    ctx_count, fsdp_count, partial, mixed, noise, sig, generated, noisy, out, *scratch
+):
+    place = Place(ctx_count, fsdp_count)
+    greet(place.group_targets())
+    gen_sum = scatter_sum(place, partial, *scratch[:3], scratch[3:7])
+    value = (mixed[...].astype(jnp.float32) + gen_sum).astype(jnp.bfloat16)
+    generated[...] = value
+    level = sig[:, :1]
+    noisy[...] = (
+        (1.0 - level) * value.astype(jnp.float32) + level * noise[...].astype(jnp.float32)
+    ).astype(jnp.bfloat16)
+    spread = Spread(place, noisy, out, 0, scratch[7:11], 0)
+    spread.start()
+    local = pltpu.make_async_copy(noisy, out.at[place.me], scratch[11])
+    local.start()
+    spread.forward()
+    spread.end()
+    local.wait()
+
+
+def cotangent_kernel(
+    ctx_count, fsdp_count, partial, generated, noisy, out, cotangent, *scratch
+):
+    place = Place(ctx_count, fsdp_count)
+    greet(place.group_targets() + place.ctx_targets())
+    teacher_sum = scatter_sum(place, partial, *scratch[:3], scratch[3:7])
+    real = noisy[...].astype(jnp.float32) + teacher_sum
+    cotangent[...] = (generated[...].astype(jnp.float32) - real).astype(jnp.bfloat16)
+    ctx_send, ctx_recv, local_sem = scratch[11:14]
+
+    def along(step, source):
+        return remote(
+            cotangent,
+            out.at[source * fsdp_count + place.me],
+            ctx_send.at[step],
+            ctx_recv.at[step],
+            (place.ctx_ahead(step), place.me),
+        )
+
+    for step in range(1, ctx_count):
+        along(step, place.z).start()
+    spreads = [Spread(place, cotangent, out, place.z * fsdp_count, scratch[7:11], 0)]
+    spreads[0].start()
+    local = pltpu.make_async_copy(cotangent, out.at[place.z * fsdp_count + place.me], local_sem)
+    local.start()
+    for step in range(1, ctx_count):
+        source = place.ctx_behind(step)
+        along(step, source).wait_recv()
+        row = source * fsdp_count
+        spreads.append(
+            Spread(place, out.at[row + place.me], out, row, scratch[7:11], step)
+        )
+        spreads[-1].start()
+        spreads[-2].forward()
+    spreads[-1].forward()
+    for spread in spreads:
+        spread.end()
+    for step in range(1, ctx_count):
+        along(step, place.z).wait_send()
+    local.wait()
+
+
+def renoise(partial, mixed, noise, sig, ctx_count, fsdp_count, identity):
+    rows, columns = mixed.shape
+    chips = fsdp_count // 2
+    vmem = pl.BlockSpec(memory_space=pltpu.VMEM)
+    block = jax.ShapeDtypeStruct((rows, columns), jnp.bfloat16)
+    generated, noisy, gathered = pl.pallas_call(
+        functools.partial(renoise_kernel, ctx_count, fsdp_count),
+        out_shape=(
+            block,
+            block,
+            jax.ShapeDtypeStruct((fsdp_count, rows, columns), jnp.bfloat16),
+        ),
+        in_specs=[vmem] * 4,
+        out_specs=(vmem, vmem, pl.BlockSpec(memory_space=pl.ANY)),
+        scratch_shapes=scatter_scratch(chips, rows, columns)
+        + spread_sems(1, chips)
+        + [pltpu.SemaphoreType.DMA],
+        compiler_params=pltpu.CompilerParams(
+            collective_id=identity, has_side_effects=True, vmem_limit_bytes=VMEM_BYTES
+        ),
+    )(
+        partial.reshape(fsdp_count, rows, columns),
+        mixed,
+        noise,
+        jnp.broadcast_to(sig, (rows, 128)),
+    )
+    return generated, noisy, gathered.reshape(fsdp_count * rows, columns)
+
+
+def all_cotangents(partial, generated, noisy, ctx_count, fsdp_count, identity):
+    rows, columns = noisy.shape
+    chips = fsdp_count // 2
+    vmem = pl.BlockSpec(memory_space=pltpu.VMEM)
+    devices = ctx_count * fsdp_count
+    gathered = pl.pallas_call(
+        functools.partial(cotangent_kernel, ctx_count, fsdp_count),
+        out_shape=jax.ShapeDtypeStruct((devices, rows, columns), jnp.bfloat16),
+        in_specs=[vmem] * 3,
+        out_specs=pl.BlockSpec(memory_space=pl.ANY),
+        scratch_shapes=[pltpu.VMEM((rows, columns), jnp.bfloat16)]
+        + scatter_scratch(chips, rows, columns)
+        + spread_sems(ctx_count, chips)
+        + [
+            pltpu.SemaphoreType.DMA((ctx_count,)),
+            pltpu.SemaphoreType.DMA((ctx_count,)),
+            pltpu.SemaphoreType.DMA,
+        ],
+        compiler_params=pltpu.CompilerParams(
+            collective_id=identity, has_side_effects=True, vmem_limit_bytes=VMEM_BYTES
+        ),
+    )(partial.reshape(fsdp_count, rows, columns), generated, noisy)
+    return gathered.reshape(devices * rows, columns)
 
 
 def per_device(
@@ -101,12 +450,12 @@
     )
     gen_stack = jnp.concatenate([gen_query, gen_key, gen_value], axis=1)
     projected = jnp.dot(
-        normed(lax.all_gather(mixed, "fsdp", axis=0, tiled=True)),
+        normed(group_gather(mixed, ctx_count, fsdp_count, 0)),
         gen_stack,
         preferred_element_type=jnp.float32,
     ).astype(jnp.bfloat16)
     query_heads = projected[:, :width].reshape(block_rows, heads, HEAD)
-    span = lax.all_gather(projected[:, width:], "ctx", axis=0, tiled=True)
+    span = ctx_gather(projected[:, width:], ctx_count, fsdp_count, 1)
     slots_all = slots * ctx_count
     cached_keys = cache[:, :slots].reshape(slots_all, heads, HEAD)
     cached_values = cache[:, slots : 2 * slots].reshape(slots_all, heads, HEAD)
@@ -123,26 +472,24 @@
         ),
     )
     attn_all = lax.all_gather(attn, "ctx", axis=0, tiled=True)
-    gen_sum = lax.psum_scatter(
+    sig_teacher = sigmas(steps_teacher, offset, tok_dev, total)
+    generated, noisy, noisy_group = renoise(
         jnp.dot(attn, gen_out, preferred_element_type=jnp.float32).astype(jnp.bfloat16),
-        "fsdp",
-        scatter_dimension=0,
-        tiled=True,
-    ).astype(jnp.float32)
-    generated = (mixed.astype(jnp.float32) + gen_sum).astype(jnp.bfloat16)
-    sig_teacher = sigmas(steps_teacher, offset, tok_dev, total)
-    noisy = (
-        (1.0 - sig_teacher) * generated.astype(jnp.float32)
-        + sig_teacher * noise_two.astype(jnp.float32)
-    ).astype(jnp.bfloat16)
+        mixed,
+        noise_two,
+        sig_teacher,
+        ctx_count,
+        fsdp_count,
+        2,
+    )
     teacher_stack = jnp.concatenate([teacher_query, teacher_key, teacher_value], axis=1)
     teacher_proj = jnp.dot(
-        normed(lax.all_gather(noisy, "fsdp", axis=0, tiled=True)),
+        normed(noisy_group),
         teacher_stack,
         preferred_element_type=jnp.float32,
     ).astype(jnp.bfloat16)
     teacher_heads = teacher_proj[:, :width].reshape(block_rows, heads, HEAD)
-    t_span = lax.all_gather(teacher_proj[:, width:], "ctx", axis=0, tiled=True)
+    t_span = ctx_gather(teacher_proj[:, width:], ctx_count, fsdp_count, 3)
     teacher_attn = attend(
         teacher_heads,
         (
@@ -153,17 +500,17 @@
             ),
         ),
     )
-    teacher_sum = lax.psum_scatter(
+    cotangents = all_cotangents(
         jnp.dot(teacher_attn, teacher_out, preferred_element_type=jnp.float32).astype(jnp.bfloat16),
-        "fsdp",
-        scatter_dimension=0,
-        tiled=True,
-    ).astype(jnp.float32)
-    real = noisy.astype(jnp.float32) + teacher_sum
-    cotangent = (generated.astype(jnp.float32) - real).astype(jnp.bfloat16)
+        generated,
+        noisy,
+        ctx_count,
+        fsdp_count,
+        4,
+    )
     grad_out = lax.dot_general(
         attn_all,
-        lax.all_gather(cotangent, ("ctx", "fsdp"), axis=0, tiled=True),
+        cotangents,
         (((0,), (0,)), ((), ())),
         preferred_element_type=jnp.float32,
     ).astype(jnp.bfloat16)

time: 477 us -> 334 us (0.70)
  waiting for transfers between devices: 386 us -> 0.04 us
  Pallas kernels: 0 us -> 250 us
  other arithmetic: 16.6 us -> 10.1 us
    pallas_call x0 -> x5, Pallas kernels: none -> 250 us  [the longest x2 99.6 us: ctx_gather(): pl.pallas_call(functools.partial(ctx_kernel, ctx_count, fsdp_count), out_...]
    all_gather x5 -> x0, waiting for transfers between devices: 234 us -> none  [the longest x1 88.5 us: per_device(): lax.all_gather(cotangent, ('ctx', 'fsdp'), axis=0, tiled=True)]
    reduce_scatter x2 -> x0, waiting for transfers between devices: 84.2 us -> none  [the longest x1 42.5 us: per_device(): lax.psum_scatter(jnp.dot(attn, gen_out, preferred_element_type=jnp.float3...]
    all_gather x1, waiting for transfers between devices: 37.4 us -> 0.01 us  [per_device(): lax.all_gather(jnp.concatenate([cache_key, cache_value, flags], axis=0),...]
    all_gather x1, waiting for transfers between devices: 29.9 us -> 0.01 us  [per_device(): attn_all = lax.all_gather(attn, 'ctx', axis=0, tiled=True)]
  transfers between devices with their start and end apart: 9 -> 2, of which waited for: 9 -> 0; matrix products, arithmetic and copies ran while one was open for 5% -> 12% of each run, Pallas kernels for 0% -> 75%
where the time goes in v2:
time: 334 us; the launch traced here: 333 us
  Pallas kernels  250 us (75%)
  matrix products  40.6 us (12%)
  local copies, waits for them, and re-layouts  17.4 us (5%)
  between operations  15 us (4%)
  other arithmetic  10.1 us (3%)
    pallas_call x2, Pallas kernels, ctx_gather(): pl.pallas_call(functools.partial(ctx_kernel, ctx_count, fsdp_count), out_...  99.6 us
    pallas_call x1, Pallas kernels, all_cotangents(): pl.pallas_call(functools.partial(cotangent_kernel, ctx_count, fsdp_count)...  91.2 us
    pallas_call x1, Pallas kernels, renoise(): pl.pallas_call(functools.partial(renoise_kernel, ctx_count, fsdp_count),...  38.5 us
    pallas_call x1, Pallas kernels, group_gather(): pl.pallas_call(functools.partial(group_kernel, ctx_count, fsdp_count), ou...  20.8 us
    dot_general x1, matrix products, per_device(): lax.dot_general(attn_all, cotangents, (((0,), (0,)), ((), ())), preferred...  10 us
    unnamed x25, local copies, waits for them, and re-layouts  9.85 us
    dot_general x1, matrix products, per_device(): jnp.dot(normed(noisy_group), teacher_stack, preferred_element_type=jnp.fl...  8.3 us
    dot_general x1, matrix products, per_device(): jnp.dot(normed(group_gather(mixed, ctx_count, fsdp_count, 0)), gen_stack,...  8.16 us
  transfers between devices with their start and end apart: 2, of which 0 were waited for; matrix products, arithmetic and copies ran while one was open for 12% of the time, Pallas kernels for 75%

profile of v2, /device:TPU:0, one launch (start us, length us, event | category | flops | bytes accessed | tf_op | source)
XLA Modules:
  0.0 333.2 jit_solution(15675107185290855319)
XLA Ops:
  7.9 0.7 broadcast_compare_fusion
  8.6 1.9 pad_maximum_fusion
  10.5 0.7 add_divide_fusion
  11.2 0.1 select_reduce_fusion
  11.3 1.3 add_convert_fusion.src.mixed
  12.6 20.8 %shard_map.176 = bf16[8,32,5120]{2,1,0:T(8,128)(2,1)S(1)} custom-call(bf16[32,5120]{1,0:T(8,128)(2,1)S(1)} %add_convert_fusion.src.mixed), custom_call_target="tpu_custom_call" | custom-call | tf_op jit(solution)/shard_map/pallas_call | solution.py:190
  33.4 0.6 multiply_reduce_fusion.1
  34.0 0.1 rsqrt.23
  34.1 0.7 fusion.13
  34.8 8.2 %fusion.24 = bf16[256,1536]{1,0:T(8,128)(2,1)S(1)} fusion(bf16[256,5120]{1,0:T(8,128)(2,1)S(1)} %fusion.13, bf16[5120,512]{1,0:T(8,128)(2,1)} %param.28, bf16[5120,512]{1,0:T(8,128)(2,1)} %param.27, bf16[5120,512]{1,0:T(8,128)(2,1)} %param.26), kind=kOutput, calls=%fused_computation.35 | convolution fusion | flops 4074110976 | bytes 19136512 | tf_op jit(solution)/shard_map/dot_general | solution.py:452
  43.0 0.1 slice.52.src
  43.0 51.0 %shard_map.177 = bf16[4,256,1024]{2,1,0:T(8,128)(2,1)S(1)} custom-call(bf16[256,1024]{1,0:T(8,128)(2,1)S(1)} %slice.52.src), custom_call_target="tpu_custom_call" | custom-call | tf_op jit(solution)/shard_map/pallas_call | solution.py:229
  94.0 0.2 fusion.79
  94.2 1.3 copy.42
  95.5 0.5 copy.50
  96.0 2.7 multiply_reduce_fusion.3
  98.7 0.8 slice_bitcast_fusion.2
  99.6 1.8 fusion.77
  101.4 1.1 reshape.165
  102.6 0.3 reshape.148
  102.9 0.9 fusion.14
  103.8 0.3 copy-done.6
  104.1 1.2 fusion.35
  105.3 1.0 copy-done.4
  106.3 1.9 fusion.15
  108.2 1.7 fusion.59
  110.0 4.2 %convolution_convert_fusion.2 = bf16[256,5120]{1,0:T(8,128)(2,1)S(1)} fusion(bf16[256,512]{0,1:T(8,128)(2,1)} %bitcast.88, bf16[512,5120]{1,0:T(8,128)(2,1)} %param.29), kind=kOutput, calls=%fused_computation.14 | convolution fusion | flops 1343488000 | bytes 8126464 | tf_op jit(solution)/shard_map/dot_general | solution.py:477
  114.2 0.1 broadcast_in_dim.23.sig
  114.3 38.5 %shard_map.178 = (bf16[32,5120]{1,0:T(8,128)(2,1)S(1)}, bf16[32,5120]{1,0:T(8,128)(2,1)S(1)}, bf16[8,32,5120]{2,1,0:T(8,128)(2,1)S(1)}) custom-call(bf16[8,32,5120]{2,1,0:T(8,128)(2,1)S(1)} %bitcast.77, bf16[32,5120]{1,0:T(8,128)(2,1)S(1)} %add_convert_fusion.src.mixed, bf16[32,5120]{1,0:T(8,128)(2,1)S(1)} %copy-done.1, f32[32,128]{1,0:T(8,128)S(1)} %broadcast_in_dim.23.sig), custom_call_target="tpu_custom_call" | custom-call | tf_op jit(solution)/shard_map/pallas_call | solution.py:364
  152.7 0.7 copy-done.2
  153.4 0.6 multiply_reduce_fusion
  154.1 0.1 rsqrt.25
  154.1 0.7 fusion.12
  154.8 8.3 %fusion.21 = bf16[256,1536]{1,0:T(8,128)(2,1)S(1)} fusion(bf16[256,5120]{1,0:T(8,128)(2,1)S(1)} %fusion.12, bf16[5120,512]{1,0:T(8,128)(2,1)} %param.32, bf16[5120,512]{1,0:T(8,128)(2,1)} %param.31, bf16[5120,512]{1,0:T(8,128)(2,1)} %param.30), kind=kOutput, calls=%fused_computation.34 | convolution fusion | flops 4074110976 | bytes 19136512 | tf_op jit(solution)/shard_map/dot_general | solution.py:486
  163.1 0.1 slice.57.src
  163.2 48.6 %shard_map.179 = bf16[4,256,1024]{2,1,0:T(8,128)(2,1)S(1)} custom-call(bf16[256,1024]{1,0:T(8,128)(2,1)S(1)} %slice.57.src), custom_call_target="tpu_custom_call" | custom-call | tf_op jit(solution)/shard_map/pallas_call | solution.py:229
  211.8 1.1 fusion.78
  213.0 1.5 copy.51
  214.5 1.3 copy.46
  215.8 0.8 multiply_reduce_fusion.2
  216.6 0.9 fusion.17
  217.5 1.0 fusion.50
  218.6 0.2 slice-done.1
  218.8 1.6 convolution_convert_fusion.1
  220.4 91.2 %shard_map.180 = bf16[32,32,5120]{2,1,0:T(8,128)(2,1)S(1)} custom-call(bf16[8,32,5120]{2,1,0:T(8,128)(2,1)S(1)} %bitcast.78, bf16[32,5120]{1,0:T(8,128)(2,1)S(1)} %get-tuple-element.28.generated, bf16[32,5120]{1,0:T(8,128)(2,1)S(1)} %copy-done.3), custom_call_target="tpu_custom_call" | custom-call | tf_op jit(solution)/shard_map/pallas_call | solution.py:393
  311.6 4.0 %copy-done = bf16[32,32,5120]{2,1,0:T(8,128)(2,1)} copy-done((bf16[32,32,5120]{2,1,0:T(8,128)(2,1)}, bf16[32,32,5120]{2,1,0:T(8,128)(2,1)S(1)}, u32[]{:S(2)}) %copy-start) | copy-done | bytes 10485784
  315.6 10.0 %convolution_convert_fusion = bf16[512,5120]{1,0:T(8,128)(2,1)} fusion(bf16[1024,512]{0,1:T(8,128)(2,1)} %all-gather.4.cloned.1.call-done, bf16[1024,5120]{1,0:T(8,128)(2,1)} %bitcast.76), kind=kOutput, calls=%fused_computation.12 | convolution fusion | flops 5371330560 | bytes 16777216 | tf_op jit(solution)/shard_map/dot_general | solution.py:511
  325.6 0.7 copy.81
  (33 shorter events, 0.3 us)
Async XLA Ops:
  7.2 91.6 %all-gather.6.cloned.1.call-start = ((), (), s32[]{:S(2)}) async-start(), calls=%async_computation.1 | async-start | bytes 2703360 | tf_op jit(solution)/shard_map/all_gather | solution.py:448
  10.5 305.1 %all-gather.4.cloned.1.call-start = ((), (), s32[]{:S(2)}) async-start(), calls=%async_computation | async-start | bytes 1310720 | tf_op jit(solution)/shard_map/all_gather | solution.py:474
  102.9 1.2 copy-start.6
  104.1 2.2 copy-start.4
  106.3 1.9 copy-start.5
  110.0 4.3 %copy-start.1 = (bf16[32,5120]{1,0:T(8,128)(2,1)S(1)}, bf16[32,5120]{1,0:T(8,128)(2,1)}, u32[]{:S(2)}) copy-start(bf16[32,5120]{1,0:T(8,128)(2,1)} %noise.1) | copy-start | bytes 983044
  152.7 0.7 copy-start.2
  215.8 1.7 copy-start.7
  215.8 2.8 slice-start
  216.6 2.2 slice-start.1
  218.8 1.6 copy-start.3
  311.6 4.0 %copy-start = (bf16[32,32,5120]{2,1,0:T(8,128)(2,1)}, bf16[32,32,5120]{2,1,0:T(8,128)(2,1)S(1)}, u32[]{:S(2)}) copy-start(bf16[32,32,5120]{2,1,0:T(8,128)(2,1)S(1)} %shard_map.180) | copy-start | bytes 31457284
Sparse Core Ops, SparseCore 0:
  10.6 78.5 all-gather.5
  110.1 39.9 all-gather.3

commit v3 on v2

--- a/solution.py
+++ b/solution.py
@@ -80,10 +80,20 @@
         self.core = lax.rem(self.me, 2)
         self.sibling = self.chip * 2 + 1 - self.core
 
+    def across(self, step):
+        x, y = lax.rem(self.chip, 2), lax.div(self.chip, 2)
+        x = 1 - x if step in (1, 3) else x
+        y = 1 - y if step in (2, 3) else y
+        return (y * 2 + x) * 2
+
     def ahead(self, step):
+        if self.chips == 4:
+            return self.across(step)
         return lax.rem(self.chip + step, self.chips) * 2
 
     def behind(self, step):
+        if self.chips == 4:
+            return self.across(step)
         return lax.rem(self.chip + self.chips - step, self.chips) * 2
 
     def group_targets(self):
@@ -122,7 +132,9 @@
     def __init__(self, place, src, out, row, sems, index):
         self.place, self.src, self.out, self.row = place, src, out, row
         self.send, self.recv, self.relay_send, self.relay_recv = (s.at[index] for s in sems)
-        self.relays = []
+        self.half = out.shape[1] // 2
+        self.square = place.chips == 4 and self.half % 16 == 0
+        self.direct = range(1, 3) if self.square else range(1, place.chips)
 
     def own(self, step):
         p = self.place
@@ -150,27 +162,49 @@
         )
 
     def start(self):
-        for step in list(range(1, self.place.chips)) + [0]:
+        for step in list(self.direct) + [0]:
             self.own(step).start()
 
+    def hop(self, step, origin):
+        p = self.place
+        part = pl.ds((step - 1) * self.half, self.half)
+        block = self.out.at[self.row + p.across(origin) + p.core, part]
+        return remote(
+            block,
+            block,
+            self.send.at[2 + step],
+            self.recv.at[2 + step],
+            (p.z, p.across(3 - step) + p.core),
+        )
+
     def forward(self):
-        for step in range(1, self.place.chips):
+        for step in self.direct:
             self.arrival(step).wait_recv()
+            if self.square:
+                self.hop(step, step).start()
             self.relay(step, self.place.core).start()
+
+    def corner(self):
+        if self.square:
+            self.hop(1, 3).wait_recv()
+            self.hop(2, 3).wait_recv()
+            self.relay(3, self.place.core).start()
 
     def end(self):
         p = self.place
         self.arrival(0).wait_recv()
         for step in range(1, p.chips):
             self.relay(step, 1 - p.core).wait_recv()
-        for step in range(p.chips):
+        for step in [0] + list(self.direct):
             self.own(step).wait_send()
+            if self.square and step > 0:
+                self.hop(step, step).wait_send()
         for step in range(1, p.chips):
             self.relay(step, p.core).wait_send()
 
 
 def spread_sems(parts, chips):
-    return [pltpu.SemaphoreType.DMA((parts, chips)) for _ in range(4)]
+    return [pltpu.SemaphoreType.DMA((parts, chips + 1)) for _ in range(4)]
 
 
 def group_kernel(ctx_count, fsdp_count, src, out, *sems):
@@ -181,6 +215,7 @@
     local = pltpu.make_async_copy(src, out.at[place.me], sems[4])
     local.start()
     spread.forward()
+    spread.corner()
     spread.end()
     local.wait()
 
@@ -200,27 +235,71 @@
     return gathered.reshape(fsdp_count * rows, columns)
 
 
-def ctx_kernel(ctx_count, fsdp_count, src, out, send_sem, recv_sem, local_sem):
+def ctx_kernel(
+    ctx_count, fsdp_count, src, out, right_send, right_recv, left_send, left_recv, local_sem
+):
     place = Place(ctx_count, fsdp_count)
+    z, last = place.z, ctx_count - 1
     greet(place.ctx_targets())
-
-    def copy(step, slot):
-        return remote(
-            src,
-            out.at[slot],
-            send_sem.at[step],
-            recv_sem.at[step],
-            (place.ctx_ahead(step), place.me),
-        )
-
-    for step in range(1, ctx_count):
-        copy(step, place.z).start()
-    local = pltpu.make_async_copy(src, out.at[place.z], local_sem)
+    half = src.shape[0] // 2
+    local = pltpu.make_async_copy(src, out.at[z], local_sem)
     local.start()
-    for step in range(1, ctx_count):
-        copy(step, place.ctx_behind(step)).wait_recv()
-    for step in range(1, ctx_count):
-        copy(step, place.z).wait_send()
+
+    def right(hops, part, slot):
+        rows = pl.ds(part * half, half)
+        block = src.at[rows] if hops == 0 else out.at[slot, rows]
+        return remote(
+            block,
+            out.at[slot, rows],
+            right_send.at[hops, part],
+            right_recv.at[hops, part],
+            (place.ctx_ahead(1), place.me),
+        )
+
+    def left(hops, part, slot):
+        rows = pl.ds(part * half, half)
+        block = src.at[rows] if hops == 0 else out.at[slot, rows]
+        return remote(
+            block,
+            out.at[slot, rows],
+            left_send.at[hops, part],
+            left_recv.at[hops, part],
+            (place.ctx_behind(1), place.me),
+        )
+
+    for hops in range(ctx_count):
+        for part in range(2):
+            if hops > 0:
+
+                @pl.when(z >= hops)
+                def _():
+                    right(hops - 1, part, z - hops).wait_recv()
+
+                @pl.when(z + hops <= last)
+                def _():
+                    left(hops - 1, part, z + hops).wait_recv()
+
+            if hops < last:
+
+                @pl.when(jnp.logical_and(z >= hops, z < last))
+                def _():
+                    right(hops, part, z - hops).start()
+
+                @pl.when(jnp.logical_and(z + hops <= last, z > 0))
+                def _():
+                    left(hops, part, z + hops).start()
+
+    for hops in range(last):
+        for part in range(2):
+
+            @pl.when(jnp.logical_and(z >= hops, z < last))
+            def _():
+                right(hops, part, z - hops).wait_send()
+
+            @pl.when(jnp.logical_and(z + hops <= last, z > 0))
+            def _():
+                left(hops, part, z + hops).wait_send()
+
     local.wait()
 
 
@@ -232,8 +311,10 @@
         in_specs=[pl.BlockSpec(memory_space=pl.ANY)],
         out_specs=pl.BlockSpec(memory_space=pl.ANY),
         scratch_shapes=[
-            pltpu.SemaphoreType.DMA((ctx_count,)),
-            pltpu.SemaphoreType.DMA((ctx_count,)),
+            pltpu.SemaphoreType.DMA((ctx_count, 2)),
+            pltpu.SemaphoreType.DMA((ctx_count, 2)),
+            pltpu.SemaphoreType.DMA((ctx_count, 2)),
+            pltpu.SemaphoreType.DMA((ctx_count, 2)),
             pltpu.SemaphoreType.DMA,
         ],
         compiler_params=pltpu.CompilerParams(
@@ -310,6 +391,7 @@
     local = pltpu.make_async_copy(noisy, out.at[place.me], scratch[11])
     local.start()
     spread.forward()
+    spread.corner()
     spread.end()
     local.wait()
 
@@ -348,7 +430,11 @@
         )
         spreads[-1].start()
         spreads[-2].forward()
+        if step > 1:
+            spreads[-3].corner()
     spreads[-1].forward()
+    for spread in spreads[-2:]:
+        spread.corner()
     for spread in spreads:
         spread.end()
     for step in range(1, ctx_count):

time: 334 us -> 303 us (0.907)
  Pallas kernels: 250 us -> 216 us
    pallas_call x1, Pallas kernels: 91.2 us -> 71.4 us  [all_cotangents(): pl.pallas_call(functools.partial(cotangent_kernel, ctx_count, fsdp_count)...]
    pallas_call x2, Pallas kernels: 99.6 us -> 89.8 us  [ctx_gather(): pl.pallas_call(functools.partial(ctx_kernel, ctx_count, fsdp_count), out_...]
  transfers between devices with their start and end apart: 2 -> 2, of which waited for: 0 -> 0; matrix products, arithmetic and copies ran while one was open for 12% -> 13% of each run, Pallas kernels for 75% -> 72%
where the time goes in v3:
time: 303 us; the launch traced here: 299 us
  Pallas kernels  216 us (71%)
  matrix products  40.6 us (13%)
  local copies, waits for them, and re-layouts  17.4 us (6%)
  between operations  15 us (5%)
  other arithmetic  10.1 us (3%)
    pallas_call x2, Pallas kernels, ctx_gather(): pl.pallas_call(functools.partial(ctx_kernel, ctx_count, fsdp_count), out_...  89.8 us
    pallas_call x1, Pallas kernels, all_cotangents(): pl.pallas_call(functools.partial(cotangent_kernel, ctx_count, fsdp_count)...  71.4 us
    pallas_call x1, Pallas kernels, renoise(): pl.pallas_call(functools.partial(renoise_kernel, ctx_count, fsdp_count),...  36.6 us
    pallas_call x1, Pallas kernels, group_gather(): pl.pallas_call(functools.partial(group_kernel, ctx_count, fsdp_count), ou...  18.1 us
    dot_general x1, matrix products, per_device(): lax.dot_general(attn_all, cotangents, (((0,), (0,)), ((), ())), preferred...  10 us
    unnamed x25, local copies, waits for them, and re-layouts  9.85 us
    dot_general x1, matrix products, per_device(): jnp.dot(normed(noisy_group), teacher_stack, preferred_element_type=jnp.fl...  8.3 us
    dot_general x1, matrix products, per_device(): jnp.dot(normed(group_gather(mixed, ctx_count, fsdp_count, 0)), gen_stack,...  8.16 us
  transfers between devices with their start and end apart: 2, of which 0 were waited for; matrix products, arithmetic and copies ran while one was open for 13% of the time, Pallas kernels for 72%

profile of v3, /device:TPU:0, one launch (start us, length us, event | category | flops | bytes accessed | tf_op | source)
XLA Modules:
  0.0 299.1 jit_solution(17885841611218032180)
XLA Ops:
  7.9 0.7 broadcast_compare_fusion
  8.6 1.9 pad_maximum_fusion
  10.5 0.7 add_divide_fusion
  11.2 0.1 select_reduce_fusion
  11.3 1.3 add_convert_fusion.src.mixed
  12.6 18.1 %shard_map.176 = bf16[8,32,5120]{2,1,0:T(8,128)(2,1)S(1)} custom-call(bf16[32,5120]{1,0:T(8,128)(2,1)S(1)} %add_convert_fusion.src.mixed), custom_call_target="tpu_custom_call" | custom-call | tf_op jit(solution)/shard_map/pallas_call | solution.py:225
  30.7 0.6 multiply_reduce_fusion.1
  31.3 0.1 rsqrt.23
  31.4 0.7 fusion.13
  32.1 8.2 %fusion.24 = bf16[256,1536]{1,0:T(8,128)(2,1)S(1)} fusion(bf16[256,5120]{1,0:T(8,128)(2,1)S(1)} %fusion.13, bf16[5120,512]{1,0:T(8,128)(2,1)} %param.28, bf16[5120,512]{1,0:T(8,128)(2,1)} %param.27, bf16[5120,512]{1,0:T(8,128)(2,1)} %param.26), kind=kOutput, calls=%fused_computation.35 | convolution fusion | flops 4074110976 | bytes 19136512 | tf_op jit(solution)/shard_map/dot_general | solution.py:538
  40.3 0.1 slice.52.src
  40.4 52.1 %shard_map.177 = bf16[4,256,1024]{2,1,0:T(8,128)(2,1)S(1)} custom-call(bf16[256,1024]{1,0:T(8,128)(2,1)S(1)} %slice.52.src), custom_call_target="tpu_custom_call" | custom-call | tf_op jit(solution)/shard_map/pallas_call | solution.py:308
  92.5 0.2 fusion.79
  92.7 1.3 copy.42
  94.0 0.5 copy.50
  94.5 2.7 multiply_reduce_fusion.3
  97.3 0.8 slice_bitcast_fusion.2
  98.1 1.8 fusion.77
  99.9 1.1 reshape.165
  101.1 0.3 reshape.148
  101.4 0.9 fusion.14
  102.3 0.3 copy-done.6
  102.6 1.2 fusion.35
  103.8 1.0 copy-done.4
  104.8 1.9 fusion.15
  106.8 1.7 fusion.59
  108.5 4.2 %convolution_convert_fusion.2 = bf16[256,5120]{1,0:T(8,128)(2,1)S(1)} fusion(bf16[256,512]{0,1:T(8,128)(2,1)} %bitcast.88, bf16[512,5120]{1,0:T(8,128)(2,1)} %param.29), kind=kOutput, calls=%fused_computation.14 | convolution fusion | flops 1343488000 | bytes 8126464 | tf_op jit(solution)/shard_map/dot_general | solution.py:563
  112.7 0.1 broadcast_in_dim.23.sig
  112.8 36.6 %shard_map.178 = (bf16[32,5120]{1,0:T(8,128)(2,1)S(1)}, bf16[32,5120]{1,0:T(8,128)(2,1)S(1)}, bf16[8,32,5120]{2,1,0:T(8,128)(2,1)S(1)}) custom-call(bf16[8,32,5120]{2,1,0:T(8,128)(2,1)S(1)} %bitcast.77, bf16[32,5120]{1,0:T(8,128)(2,1)S(1)} %add_convert_fusion.src.mixed, bf16[32,5120]{1,0:T(8,128)(2,1)S(1)} %copy-done.1, f32[32,128]{1,0:T(8,128)S(1)} %broadcast_in_dim.23.sig), custom_call_target="tpu_custom_call" | custom-call | tf_op jit(solution)/shard_map/pallas_call | solution.py:450
  149.4 0.7 copy-done.2
  150.1 0.6 multiply_reduce_fusion
  150.7 0.1 rsqrt.25
  150.8 0.7 fusion.12
  151.5 8.3 %fusion.21 = bf16[256,1536]{1,0:T(8,128)(2,1)S(1)} fusion(bf16[256,5120]{1,0:T(8,128)(2,1)S(1)} %fusion.12, bf16[5120,512]{1,0:T(8,128)(2,1)} %param.32, bf16[5120,512]{1,0:T(8,128)(2,1)} %param.31, bf16[5120,512]{1,0:T(8,128)(2,1)} %param.30), kind=kOutput, calls=%fused_computation.34 | convolution fusion | flops 4074110976 | bytes 19136512 | tf_op jit(solution)/shard_map/dot_general | solution.py:572
  159.8 0.1 slice.57.src
  159.8 37.7 %shard_map.179 = bf16[4,256,1024]{2,1,0:T(8,128)(2,1)S(1)} custom-call(bf16[256,1024]{1,0:T(8,128)(2,1)S(1)} %slice.57.src), custom_call_target="tpu_custom_call" | custom-call | tf_op jit(solution)/shard_map/pallas_call | solution.py:308
  197.6 1.1 fusion.78
  198.7 1.5 copy.51
  200.2 1.3 copy.46
  201.5 0.8 multiply_reduce_fusion.2
  202.3 0.9 fusion.17
  203.2 1.0 fusion.50
  204.3 0.2 slice-done.1
  204.5 1.6 convolution_convert_fusion.1
  206.1 71.4 %shard_map.180 = bf16[32,32,5120]{2,1,0:T(8,128)(2,1)S(1)} custom-call(bf16[8,32,5120]{2,1,0:T(8,128)(2,1)S(1)} %bitcast.78, bf16[32,5120]{1,0:T(8,128)(2,1)S(1)} %get-tuple-element.28.generated, bf16[32,5120]{1,0:T(8,128)(2,1)S(1)} %copy-done.3), custom_call_target="tpu_custom_call" | custom-call | tf_op jit(solution)/shard_map/pallas_call | solution.py:479
  277.5 4.0 %copy-done = bf16[32,32,5120]{2,1,0:T(8,128)(2,1)} copy-done((bf16[32,32,5120]{2,1,0:T(8,128)(2,1)}, bf16[32,32,5120]{2,1,0:T(8,128)(2,1)S(1)}, u32[]{:S(2)}) %copy-start) | copy-done | bytes 10485784
  281.5 10.0 %convolution_convert_fusion = bf16[512,5120]{1,0:T(8,128)(2,1)} fusion(bf16[1024,512]{0,1:T(8,128)(2,1)} %all-gather.4.cloned.1.call-done, bf16[1024,5120]{1,0:T(8,128)(2,1)} %bitcast.76), kind=kOutput, calls=%fused_computation.12 | convolution fusion | flops 5371330560 | bytes 16777216 | tf_op jit(solution)/shard_map/dot_general | solution.py:597
  291.5 0.7 copy.81
  (33 shorter events, 0.3 us)
Async XLA Ops:
  7.2 90.1 %all-gather.6.cloned.1.call-start = ((), (), s32[]{:S(2)}) async-start(), calls=%async_computation.1 | async-start | bytes 2703360 | tf_op jit(solution)/shard_map/all_gather | solution.py:534
  10.5 271.0 %all-gather.4.cloned.1.call-start = ((), (), s32[]{:S(2)}) async-start(), calls=%async_computation | async-start | bytes 1310720 | tf_op jit(solution)/shard_map/all_gather | solution.py:560
  101.4 1.2 copy-start.6
  102.6 2.2 copy-start.4
  104.8 1.9 copy-start.5
  108.5 4.3 %copy-start.1 = (bf16[32,5120]{1,0:T(8,128)(2,1)S(1)}, bf16[32,5120]{1,0:T(8,128)(2,1)}, u32[]{:S(2)}) copy-start(bf16[32,5120]{1,0:T(8,128)(2,1)} %noise.1) | copy-start | bytes 983044
  149.4 0.7 copy-start.2
  201.5 1.7 copy-start.7
  201.5 2.8 slice-start
  202.3 2.2 slice-start.1
  204.5 1.6 copy-start.3
  277.5 4.0 %copy-start = (bf16[32,32,5120]{2,1,0:T(8,128)(2,1)}, bf16[32,32,5120]{2,1,0:T(8,128)(2,1)S(1)}, u32[]{:S(2)}) copy-start(bf16[32,32,5120]{2,1,0:T(8,128)(2,1)S(1)} %shard_map.180) | copy-start | bytes 31457284
Sparse Core Ops, SparseCore 0:
  10.6 57.3 all-gather.5
  108.6 30.1 all-gather.3

commit v4 on v3

--- a/solution.py
+++ b/solution.py
@@ -236,7 +236,7 @@
 
 
 def ctx_kernel(
-    ctx_count, fsdp_count, src, out, right_send, right_recv, left_send, left_recv, local_sem
+    ctx_count, fsdp_count, src, wide, weight, out, query, right_send, right_recv, left_send, left_recv, local_sem
 ):
     place = Place(ctx_count, fsdp_count)
     z, last = place.z, ctx_count - 1
@@ -289,6 +289,11 @@
                 def _():
                     left(hops, part, z + hops).start()
 
+        if hops == 0:
+            query[...] = jnp.dot(
+                wide[...], weight[...], preferred_element_type=jnp.float32
+            ).astype(jnp.bfloat16)
+
     for hops in range(last):
         for part in range(2):
 
@@ -303,13 +308,17 @@
     local.wait()
 
 
-def ctx_gather(values, ctx_count, fsdp_count, identity):
+def ctx_gather(values, wide, weight, ctx_count, fsdp_count, identity):
     rows, columns = values.shape
-    gathered = pl.pallas_call(
+    vmem = pl.BlockSpec(memory_space=pltpu.VMEM)
+    gathered, query = pl.pallas_call(
         functools.partial(ctx_kernel, ctx_count, fsdp_count),
-        out_shape=jax.ShapeDtypeStruct((ctx_count, rows, columns), values.dtype),
-        in_specs=[pl.BlockSpec(memory_space=pl.ANY)],
-        out_specs=pl.BlockSpec(memory_space=pl.ANY),
+        out_shape=(
+            jax.ShapeDtypeStruct((ctx_count, rows, columns), values.dtype),
+            jax.ShapeDtypeStruct((rows, weight.shape[1]), values.dtype),
+        ),
+        in_specs=[pl.BlockSpec(memory_space=pl.ANY), vmem, vmem],
+        out_specs=(pl.BlockSpec(memory_space=pl.ANY), vmem),
         scratch_shapes=[
             pltpu.SemaphoreType.DMA((ctx_count, 2)),
             pltpu.SemaphoreType.DMA((ctx_count, 2)),
@@ -320,8 +329,8 @@
         compiler_params=pltpu.CompilerParams(
             collective_id=identity, has_side_effects=True, vmem_limit_bytes=VMEM_BYTES
         ),
-    )(values)
-    return gathered.reshape(ctx_count * rows, columns)
+    )(values, wide, weight)
+    return gathered.reshape(ctx_count * rows, columns), query
 
 
 def scatter_sum(place, partial, pair, stage, inbox, sems):
@@ -534,14 +543,15 @@
     cache = lax.all_gather(
         jnp.concatenate([cache_key, cache_value, flags], axis=0), "ctx", axis=0, tiled=False
     )
-    gen_stack = jnp.concatenate([gen_query, gen_key, gen_value], axis=1)
+    gen_stack = jnp.concatenate([gen_key, gen_value], axis=1)
+    wide = normed(group_gather(mixed, ctx_count, fsdp_count, 0))
     projected = jnp.dot(
-        normed(group_gather(mixed, ctx_count, fsdp_count, 0)),
+        wide,
         gen_stack,
         preferred_element_type=jnp.float32,
     ).astype(jnp.bfloat16)
-    query_heads = projected[:, :width].reshape(block_rows, heads, HEAD)
-    span = ctx_gather(projected[:, width:], ctx_count, fsdp_count, 1)
+    span, query = ctx_gather(projected, wide, gen_query, ctx_count, fsdp_count, 1)
+    query_heads = query.reshape(block_rows, heads, HEAD)
     slots_all = slots * ctx_count
     cached_keys = cache[:, :slots].reshape(slots_all, heads, HEAD)
     cached_values = cache[:, slots : 2 * slots].reshape(slots_all, heads, HEAD)
@@ -568,14 +578,17 @@
         fsdp_count,
         2,
     )
-    teacher_stack = jnp.concatenate([teacher_query, teacher_key, teacher_value], axis=1)
+    teacher_stack = jnp.concatenate([teacher_key, teacher_value], axis=1)
+    t_wide = normed(noisy_group)
     teacher_proj = jnp.dot(
-        normed(noisy_group),
+        t_wide,
         teacher_stack,
         preferred_element_type=jnp.float32,
     ).astype(jnp.bfloat16)
-    teacher_heads = teacher_proj[:, :width].reshape(block_rows, heads, HEAD)
-    t_span = ctx_gather(teacher_proj[:, width:], ctx_count, fsdp_count, 3)
+    t_span, t_query = ctx_gather(
+        teacher_proj, t_wide, teacher_query, ctx_count, fsdp_count, 3
+    )
+    teacher_heads = t_query.reshape(block_rows, heads, HEAD)
     teacher_attn = attend(
         teacher_heads,
         (

time: 303 us -> 301 us (level)
  matrix products: 40.6 us -> 36.3 us
    dot_general x2, matrix products: 16.5 us -> 12.1 us  [the longest x1 6.1 us: per_device(): jnp.dot(wide, gen_stack, preferred_element_type=jnp.float32)]
    unnamed x25 -> x33, local copies, waits for them, and re-layouts: 9.85 us -> 9.87 us
  transfers between devices with their start and end apart: 2 -> 2, of which waited for: 0 -> 0; matrix products, arithmetic and copies ran while one was open for 13% -> 12% of each run, Pallas kernels for 72% -> 73%
where the time goes in v4:
time: 301 us; the launch traced here: 297 us
  Pallas kernels  218 us (72%)
  matrix products  36.3 us (12%)
  local copies, waits for them, and re-layouts  17.2 us (6%)
  between operations  15 us (5%)
  other arithmetic  10.1 us (3%)
    pallas_call x2, Pallas kernels, ctx_gather(): pl.pallas_call(functools.partial(ctx_kernel, ctx_count, fsdp_count), out_...  91.9 us
    pallas_call x1, Pallas kernels, all_cotangents(): pl.pallas_call(functools.partial(cotangent_kernel, ctx_count, fsdp_count)...  71.3 us
    pallas_call x1, Pallas kernels, renoise(): pl.pallas_call(functools.partial(renoise_kernel, ctx_count, fsdp_count),...  36.6 us
    pallas_call x1, Pallas kernels, group_gather(): pl.pallas_call(functools.partial(group_kernel, ctx_count, fsdp_count), ou...  18.1 us
    dot_general x1, matrix products, per_device(): lax.dot_general(attn_all, cotangents, (((0,), (0,)), ((), ())), preferred...  10 us
    unnamed x33, local copies, waits for them, and re-layouts  9.87 us
    dot_general x1, matrix products, per_device(): jnp.dot(wide, gen_stack, preferred_element_type=jnp.float32)  6.1 us
    dot_general x1, matrix products, per_device(): jnp.dot(t_wide, teacher_stack, preferred_element_type=jnp.float32)  6.03 us
  transfers between devices with their start and end apart: 2, of which 0 were waited for; matrix products, arithmetic and copies ran while one was open for 12% of the time, Pallas kernels for 73%

profile of v4, /device:TPU:0, one launch (start us, length us, event | category | flops | bytes accessed | tf_op | source)
XLA Modules:
  0.0 296.7 jit_solution(5815197231274768469)
XLA Ops:
  7.9 0.7 broadcast_compare_fusion
  8.6 1.9 pad_maximum_fusion
  10.5 0.0 all-gather.4.cloned.1.call-start
  10.6 0.7 add_divide_fusion
  11.2 0.1 select_reduce_fusion
  11.3 1.3 add_convert_fusion.src.mixed
  12.6 18.1 %shard_map.176 = bf16[8,32,5120]{2,1,0:T(8,128)(2,1)S(1)} custom-call(bf16[32,5120]{1,0:T(8,128)(2,1)S(1)} %add_convert_fusion.src.mixed), custom_call_target="tpu_custom_call" | custom-call | tf_op jit(solution)/shard_map/pallas_call | solution.py:225
  30.8 0.6 multiply_reduce_fusion.1
  31.4 0.1 rsqrt.23
  31.4 0.7 fusion.9.wide
  32.2 6.1 %fusion.31.src = bf16[256,1024]{1,0:T(8,128)(2,1)S(1)} fusion(bf16[256,5120]{1,0:T(8,128)(2,1)S(1)} %fusion.9.wide, bf16[5120,512]{1,0:T(8,128)(2,1)} %param.28, bf16[5120,512]{1,0:T(8,128)(2,1)} %param.27), kind=kOutput, calls=%fused_computation.39 | convolution fusion | flops 2705588224 | bytes 13631488 | tf_op jit(solution)/shard_map/dot_general | solution.py:548
  38.3 54.2 %shard_map.177 = (bf16[4,256,1024]{2,1,0:T(8,128)(2,1)S(1)}, bf16[256,512]{1,0:T(8,128)(2,1)S(1)}) custom-call(bf16[256,1024]{1,0:T(8,128)(2,1)S(1)} %fusion.31.src, bf16[256,5120]{1,0:T(8,128)(2,1)S(1)} %fusion.9.wide, bf16[5120,512]{1,0:T(8,128)(2,1)S(1)} %bitcast.81), custom_call_target="tpu_custom_call" | custom-call | tf_op jit(solution)/shard_map/pallas_call | solution.py:314
  92.5 0.2 fusion.75
  92.7 1.3 copy.42
  94.0 0.5 copy.50
  94.6 2.7 multiply_reduce_fusion.3
  97.3 0.8 slice_bitcast_fusion
  98.1 1.8 fusion.73
  99.9 1.1 reshape.165
  101.0 0.1 copy.54
  101.1 0.3 reshape.148
  101.4 0.9 fusion.10
  102.3 0.3 copy-done.6
  102.6 1.2 fusion.25
  103.8 1.0 copy-done.4
  104.8 1.9 fusion.11
  106.8 1.7 fusion.55
  108.5 4.2 %convolution_convert_fusion.2 = bf16[256,5120]{1,0:T(8,128)(2,1)S(1)} fusion(bf16[256,512]{0,1:T(8,128)(2,1)} %bitcast.93, bf16[512,5120]{1,0:T(8,128)(2,1)} %param.29), kind=kOutput, calls=%fused_computation.10 | convolution fusion | flops 1343488000 | bytes 8126464 | tf_op jit(solution)/shard_map/dot_general | solution.py:573
  112.7 0.1 broadcast_in_dim.23.sig
  112.8 36.6 %shard_map.178 = (bf16[32,5120]{1,0:T(8,128)(2,1)S(1)}, bf16[32,5120]{1,0:T(8,128)(2,1)S(1)}, bf16[8,32,5120]{2,1,0:T(8,128)(2,1)S(1)}) custom-call(bf16[8,32,5120]{2,1,0:T(8,128)(2,1)S(1)} %bitcast.78, bf16[32,5120]{1,0:T(8,128)(2,1)S(1)} %add_convert_fusion.src.mixed, bf16[32,5120]{1,0:T(8,128)(2,1)S(1)} %copy-done.1, f32[32,128]{1,0:T(8,128)S(1)} %broadcast_in_dim.23.sig), custom_call_target="tpu_custom_call" | custom-call | tf_op jit(solution)/shard_map/pallas_call | solution.py:459
  149.4 0.7 copy-done.2
  150.1 0.6 multiply_reduce_fusion
  150.7 0.1 rsqrt.25
  150.8 0.7 fusion.8.wide
  151.5 6.0 %fusion.28.src = bf16[256,1024]{1,0:T(8,128)(2,1)S(1)} fusion(bf16[256,5120]{1,0:T(8,128)(2,1)S(1)} %fusion.8.wide, bf16[5120,512]{1,0:T(8,128)(2,1)} %param.32, bf16[5120,512]{1,0:T(8,128)(2,1)} %param.31), kind=kOutput, calls=%fused_computation.38 | convolution fusion | flops 2705588224 | bytes 13631488 | tf_op jit(solution)/shard_map/dot_general | solution.py:583
  157.6 37.7 %shard_map.179 = (bf16[4,256,1024]{2,1,0:T(8,128)(2,1)S(1)}, bf16[256,512]{1,0:T(8,128)(2,1)S(1)}) custom-call(bf16[256,1024]{1,0:T(8,128)(2,1)S(1)} %fusion.28.src, bf16[256,5120]{1,0:T(8,128)(2,1)S(1)} %fusion.8.wide, bf16[5120,512]{1,0:T(8,128)(2,1)S(1)} %bitcast.83), custom_call_target="tpu_custom_call" | custom-call | tf_op jit(solution)/shard_map/pallas_call | solution.py:314
  195.3 1.1 fusion.74
  196.4 1.5 copy.51
  197.9 1.3 copy.46
  199.2 0.8 multiply_reduce_fusion.2
  200.0 0.9 fusion.13
  200.9 1.0 fusion.46
  202.0 0.2 slice-done.5
  202.2 1.6 convolution_convert_fusion.1
  203.8 71.3 %shard_map.180 = bf16[32,32,5120]{2,1,0:T(8,128)(2,1)S(1)} custom-call(bf16[8,32,5120]{2,1,0:T(8,128)(2,1)S(1)} %bitcast.79, bf16[32,5120]{1,0:T(8,128)(2,1)S(1)} %get-tuple-element.36.generated, bf16[32,5120]{1,0:T(8,128)(2,1)S(1)} %copy-done.3), custom_call_target="tpu_custom_call" | custom-call | tf_op jit(solution)/shard_map/pallas_call | solution.py:488
  275.1 4.0 %copy-done = bf16[32,32,5120]{2,1,0:T(8,128)(2,1)} copy-done((bf16[32,32,5120]{2,1,0:T(8,128)(2,1)}, bf16[32,32,5120]{2,1,0:T(8,128)(2,1)S(1)}, u32[]{:S(2)}) %copy-start) | copy-done | bytes 10485784
  279.1 10.0 %convolution_convert_fusion = bf16[512,5120]{1,0:T(8,128)(2,1)} fusion(bf16[1024,512]{0,1:T(8,128)(2,1)} %all-gather.4.cloned.1.call-done, bf16[1024,5120]{1,0:T(8,128)(2,1)} %bitcast.77), kind=kOutput, calls=%fused_computation.8 | convolution fusion | flops 5371330560 | bytes 16777216 | tf_op jit(solution)/shard_map/dot_general | solution.py:610
  289.1 0.7 copy.81
  (41 shorter events, 0.2 us)
Async XLA Ops:
  7.2 90.1 %all-gather.6.cloned.1.call-start = ((), (), s32[]{:S(2)}) async-start(), calls=%async_computation.1 | async-start | bytes 2703360 | tf_op jit(solution)/shard_map/all_gather | solution.py:543
  10.5 268.6 %all-gather.4.cloned.1.call-start = ((), (), s32[]{:S(2)}) async-start(), calls=%async_computation | async-start | bytes 1310720 | tf_op jit(solution)/shard_map/all_gather | solution.py:570
  31.4 6.8 %slice-start = ((s8[5242880]{0:T(1024)(128)(4,1)}), s8[4194304]{0:T(1024)(128)(4,1)S(1)}, s32[]{:S(2)}) async-start(s8[5242880]{0:T(1024)(128)(4,1)} %bitcast.80), calls=%async_computation.2 | async-start | bytes 8388608
  32.2 6.1 %slice-start.1 = ((s8[5242880]{0:T(1024)(128)(4,1)}), s8[1048576]{0:T(1024)(128)(4,1)S(1)}, s32[]{:S(2)}) async-start(s8[5242880]{0:T(1024)(128)(4,1)} %bitcast.80), calls=%async_computation.3 | async-start | bytes 2097152
  101.4 1.2 copy-start.6
  102.6 2.2 copy-start.4
  104.8 1.9 copy-start.5
  108.5 4.3 %copy-start.1 = (bf16[32,5120]{1,0:T(8,128)(2,1)S(1)}, bf16[32,5120]{1,0:T(8,128)(2,1)}, u32[]{:S(2)}) copy-start(bf16[32,5120]{1,0:T(8,128)(2,1)} %noise.1) | copy-start | bytes 983044
  149.4 0.7 copy-start.2
  150.8 6.8 %slice-start.2 = ((s8[5242880]{0:T(1024)(128)(4,1)}), s8[4194304]{0:T(1024)(128)(4,1)S(1)}, s32[]{:S(2)}) async-start(s8[5242880]{0:T(1024)(128)(4,1)} %bitcast.82), calls=%async_computation.4 | async-start | bytes 8388608
  151.5 6.1 %slice-start.3 = ((s8[5242880]{0:T(1024)(128)(4,1)}), s8[1048576]{0:T(1024)(128)(4,1)S(1)}, s32[]{:S(2)}) async-start(s8[5242880]{0:T(1024)(128)(4,1)} %bitcast.82), calls=%async_computation.5 | async-start | bytes 2097152
  199.2 1.7 copy-start.7
  199.2 2.8 slice-start.4
  200.0 2.2 slice-start.5
  202.2 1.6 copy-start.3
  275.1 4.0 %copy-start = (bf16[32,32,5120]{2,1,0:T(8,128)(2,1)}, bf16[32,32,5120]{2,1,0:T(8,128)(2,1)S(1)}, u32[]{:S(2)}) copy-start(bf16[32,32,5120]{2,1,0:T(8,128)(2,1)S(1)} %shard_map.180) | copy-start | bytes 31457284
Sparse Core Ops, SparseCore 0:
  10.6 57.3 all-gather.5
  108.6 30.1 all-gather.3
